TPU v7x, 32 devices: a whole 2x2x4 slice. The times are simulated.
32 devices in a mesh: section: 2 (over core), fsdp: 4 (over y, x), rep: 4 (over z).
Axes of the slice: x: 2, y: 2, z: 4, core: 2. Of those that a mesh axis runs over, the one named last changes fastest.
Arguments:
- tokens: bfloat16 [2, 4, 2048, 640], P(None, 'rep', 'fsdp'), may hold values from -6 to 6
- cotangent: bfloat16 [2, 4, 2048, 640], P(None, 'rep', 'fsdp'), may hold values from -6 to 6
- lengths: int32 [2, 4, 4], P(None, 'rep'), may hold values from 1 to 1538, 2048 in all within a row
- query_weight: bfloat16 [2, 640, 1024], P('section', 'fsdp'), may hold values from -0.25 to 0.25
- key_weight: bfloat16 [2, 640, 256], P('section', 'fsdp'), may hold values from -0.25 to 0.25
- value_weight: bfloat16 [2, 640, 256], P('section', 'fsdp'), may hold values from -0.25 to 0.25
- out_weight: bfloat16 [2, 1024, 640], P('section', 'fsdp'), may hold values from -0.1875 to 0.1875
- gate_weight: bfloat16 [2, 640, 2048], P('section', 'fsdp'), may hold values from -0.25 to 0.25
- up_weight: bfloat16 [2, 640, 2048], P('section', 'fsdp'), may hold values from -0.25 to 0.25
- down_weight: bfloat16 [2, 2048, 640], P('section', 'fsdp'), may hold values from -0.125 to 0.125
- norm_gains: bfloat16 [2, 4, 640], P('section', None, 'fsdp'), may hold values from 0.5 to 1.5
- head_gains: bfloat16 [2, 2, 256], P('section', None, 'fsdp'), may hold values from 0.5 to 1.5
Outputs:
- section_out: bfloat16 [2, 2, 4, 2048, 640], P('section', None, 'rep', 'fsdp')
- input_grad: float32 [2, 2, 4, 2048, 640], P('section', None, 'rep', 'fsdp')
- grad_query_weight: float32 [2, 640, 1024], P('section', 'fsdp')
- grad_key_weight: float32 [2, 640, 256], P('section', 'fsdp')
- grad_value_weight: float32 [2, 640, 256], P('section', 'fsdp')
- grad_out_weight: float32 [2, 1024, 640], P('section', 'fsdp')
- grad_gate_weight: float32 [2, 640, 2048], P('section', 'fsdp')
- grad_up_weight: float32 [2, 640, 2048], P('section', 'fsdp')
- grad_down_weight: float32 [2, 2048, 640], P('section', 'fsdp')
- grad_norm_gains: float32 [2, 4, 640], P('section', None, 'fsdp')
- grad_head_gains: float32 [2, 2, 256], P('section', None, 'fsdp')
Inputs may be any that keep to these rules, and one draw needn't show every extreme that they name: In each micro-batch and group the 4 lengths sum to exactly 2048, so every group holds the same number of tokens, and the longest is exactly 1538.
All inputs are finite; a program needn't handle non-finite values.
Results may differ from a plain program's by a relative error of at most 0.028.
Values may be sent and summed in bfloat16 or wider, within the bound.
A program may use at most 192 MiB of HBM per device.

v0:
```python
import math

import jax
import jax.numpy as jnp
from jax import lax
from jax.sharding import PartitionSpec as P

WINDOW = 512


epsilon = 1e-06
rope_base = 10000.0
neg_fill = -1e30
gelu_coef = 0.7978845608028654


def from_behind(block, axis, distance):
    devices = range(lax.axis_size(axis))
    route = [(i - distance, i) for i in devices if i - distance in devices]
    return lax.ppermute(block, axis, route)


def rms_scale(vector, gain_vec):
    return (
        vector * lax.rsqrt(jnp.mean(vector * vector, axis=-1, keepdims=True) + epsilon) * gain_vec
    )


def gelu_tanh(vector):
    return (
        0.5 * vector * (1.0 + jnp.tanh(gelu_coef * (vector + 0.044715 * vector * vector * vector)))
    )


def geglu(gate_proj, up_proj):
    return gelu_tanh(gate_proj) * up_proj


def rotate(vector, cosine, sine_table):
    half_width = vector.shape[-1] // 2
    first_half = vector[..., :half_width]
    second_half = vector[..., half_width:]
    return jnp.concatenate(
        [
            first_half * cosine - second_half * sine_table,
            second_half * cosine + first_half * sine_table,
        ],
        axis=-1,
    )


def angle_tables(offset, width):
    frequency = jnp.exp(
        jnp.arange(width // 2, dtype=jnp.float32) * (-2.0 * math.log(rope_base) / width)
    )
    angles = offset.astype(jnp.float32)[:, None] * frequency[None, :]
    return (jnp.cos(angles), jnp.sin(angles))


def doc_layout(doc_lengths, places):
    doc_ends = jnp.cumsum(doc_lengths)
    starts = doc_ends - doc_lengths
    doc_ids = jnp.sum((places[:, None] >= doc_ends[None, :]).astype(jnp.int32), axis=1)
    numbers = jnp.arange(doc_lengths.shape[0], dtype=jnp.int32)
    first_place = jnp.sum(
        jnp.where(doc_ids[:, None] == numbers[None, :], starts[None, :], 0), axis=1
    )
    return (doc_ids, places - first_place)


def window_mask(query_docs, query_places, key_docs, key_places):
    gap_rows = query_places[:, None] - key_places[None, :]
    same_doc = query_docs[:, None] == key_docs[None, :]
    return same_doc & (key_places[None, :] >= 0) & (gap_rows >= 0) & (gap_rows < WINDOW)


def outer_dot(left, right):
    return lax.dot_general(
        left, right, (((0,), (0,)), ((), ())), preferred_element_type=jnp.float32
    )


def dot_transposed(left, right):
    return lax.dot_general(
        left, right, (((1,), (1,)), ((), ())), preferred_element_type=jnp.float32
    )


def pullback(function, first_arg, second_arg, grad_value):
    unused, back = jax.vjp(function, first_arg, second_arg)
    return back(grad_value)


def block_scores(query_heads, key_block, allowed, scale_factor):
    raw_scores = (
        jnp.einsum("hqd,kd->hqk", query_heads, key_block, preferred_element_type=jnp.float32)
        * scale_factor
    )
    return jnp.where(allowed[None], raw_scores, neg_fill)


def bit_pair():
    second_core = lax.axis_index("section") == 1
    first_bit = jnp.where(second_core, 2, 1)
    return (first_bit, 3 - first_bit)


def hop(block, stage):
    size = lax.axis_size("fsdp")
    route = []
    for core in range(2):
        bit = 1 if core == stage else 2
        for place in range(size):
            route.append((core * size + place, core * size + (place ^ bit)))
    return lax.ppermute(block, ("section", "fsdp"), route)


def swap_cores(block):
    return lax.ppermute(block, "section", [(0, 1), (1, 0)])


def ordered(mine, other, axis):
    first_core = lax.axis_index("section") == 0
    return jnp.concatenate(
        [jnp.where(first_core, mine, other), jnp.where(first_core, other, mine)], axis=axis
    )


def near_rows(block):
    return (block, hop(block, 0), hop(block, 1))


def gather_rows(pieces):
    block, near, side = pieces
    me = lax.axis_index("fsdp")
    first_bit, second_bit = bit_pair()
    far = hop(near, 1)
    held = jnp.zeros((lax.axis_size("fsdp"),) + block.shape, block.dtype)
    for piece, place in (
        (block, me),
        (near, me ^ first_bit),
        (side, me ^ second_bit),
        (far, me ^ 3),
    ):
        held = lax.dynamic_update_index_in_dim(held, piece, place, 0)
    return held


def join_rows(pair, columns):
    mine, other = pair
    mine = mine[:, None, :, columns]
    other = other[:, None, :, columns]
    whole = ordered(mine, other, 1)
    return whole.reshape(-1, whole.shape[-1])


def pick(source, place):
    return lax.dynamic_index_in_dim(source, place, 0, keepdims=False)


def row_blocks(grad):
    size = lax.axis_size("fsdp")
    return grad.reshape(size, 2, grad.shape[0] // (2 * size), grad.shape[1])


def add_cores(blocks):
    core = lax.axis_index("section")
    arrived = swap_cores(lax.dynamic_index_in_dim(blocks, 1 - core, 1, keepdims=False))
    kept = lax.dynamic_index_in_dim(blocks, core, 1, keepdims=False)
    return kept.astype(jnp.float32) + arrived.astype(jnp.float32)


def add_near(total):
    me = lax.axis_index("fsdp")
    first_bit, second_bit = bit_pair()
    near = hop(
        jnp.stack([pick(total, me ^ first_bit), pick(total, me ^ 3)]).astype(jnp.bfloat16), 0
    ).astype(jnp.float32)
    return (
        pick(total, me) + near[0],
        (pick(total, me ^ second_bit) + near[1]).astype(jnp.bfloat16),
    )


def add_far(pair):
    return (pair[0] + hop(pair[1], 1).astype(jnp.float32)).astype(jnp.bfloat16)


def layer_forward(inputs, params, layout, pending):
    qkv_weight, out_weight, gu_weight, down_weight, norm_gain, head_gain = params
    allowed_own, allowed_prior, cosine, sine_table = layout
    row_count = inputs.shape[0]
    head_size = head_gain.shape[1]
    query_width = out_weight.shape[0]
    head_count = query_width // head_size
    ff_width = down_weight.shape[0]
    scale_factor = head_size ** (-0.5)
    normed_in = rms_scale(inputs, norm_gain[0]).astype(jnp.bfloat16)
    kv_proj = jnp.dot(
        normed_in, qkv_weight[:, query_width:], preferred_element_type=jnp.float32
    )
    key_proj = kv_proj[:, :head_size]
    value_proj = kv_proj[:, head_size:].astype(jnp.bfloat16)
    key_rot = rotate(rms_scale(key_proj, head_gain[1]), cosine, sine_table).astype(jnp.bfloat16)
    prior_rows = from_behind(jnp.concatenate([key_rot, value_proj], axis=1), "fsdp", 1)
    query_proj = jnp.dot(
        normed_in, qkv_weight[:, :query_width], preferred_element_type=jnp.float32
    ).reshape(row_count, head_count, head_size)
    query_rot = rotate(
        rms_scale(query_proj, head_gain[0]), cosine[:, None, :], sine_table[:, None, :]
    ).astype(jnp.bfloat16)
    prior_keys = prior_rows[:, :head_size]
    prior_values = prior_rows[:, head_size:]
    query_heads = query_rot.transpose(1, 0, 2)
    scores_own = block_scores(query_heads, key_rot, allowed_own, scale_factor)
    scores_prior = block_scores(query_heads, prior_keys, allowed_prior, scale_factor)
    row_max = jnp.maximum(
        jnp.max(scores_own, axis=-1, keepdims=True), jnp.max(scores_prior, axis=-1, keepdims=True)
    )
    exp_own = jnp.exp(scores_own - row_max)
    exp_prior = jnp.exp(scores_prior - row_max)
    inverse = 1.0 / (
        jnp.sum(exp_own, axis=-1, keepdims=True) + jnp.sum(exp_prior, axis=-1, keepdims=True)
    )
    probs_own = (exp_own * inverse).astype(jnp.bfloat16)
    probs_prior = (exp_prior * inverse).astype(jnp.bfloat16)
    mixed_heads = jnp.einsum(
        "hqk,kd->hqd", probs_own, value_proj, preferred_element_type=jnp.float32
    ) + jnp.einsum("hqk,kd->hqd", probs_prior, prior_values, preferred_element_type=jnp.float32)
    mixed = mixed_heads.transpose(1, 0, 2).reshape(row_count, query_width).astype(jnp.bfloat16)
    attn_proj = jnp.dot(mixed, out_weight, preferred_element_type=jnp.float32)
    residual = inputs + rms_scale(attn_proj, norm_gain[1])
    residual, pending = lax.optimization_barrier((residual, pending))
    ff_in = rms_scale(residual, norm_gain[2]).astype(jnp.bfloat16)
    gate_proj = jnp.dot(ff_in, gu_weight[:, :ff_width], preferred_element_type=jnp.float32)
    up_proj = jnp.dot(ff_in, gu_weight[:, ff_width:], preferred_element_type=jnp.float32)
    hidden = geglu(gate_proj, up_proj).astype(jnp.bfloat16)
    ff_out = jnp.dot(hidden, down_weight, preferred_element_type=jnp.float32)
    outputs = residual + rms_scale(ff_out, norm_gain[3])
    kept_state = (
        inputs,
        normed_in,
        query_proj,
        key_proj,
        query_heads,
        key_rot,
        value_proj,
        prior_keys,
        prior_values,
        probs_own,
        probs_prior,
        mixed,
        attn_proj,
        residual,
        ff_in,
        gate_proj,
        up_proj,
        hidden,
        ff_out,
    )
    return (outputs, kept_state, pending)


def ff_backward(grad_out, kept_state, params):
    qkv_weight, out_weight, gu_weight, down_weight, norm_gain, head_gain = params
    (
        inputs,
        normed_in,
        query_proj,
        key_proj,
        query_heads,
        key_rot,
        value_proj,
        prior_keys,
        prior_values,
        probs_own,
        probs_prior,
        mixed,
        attn_proj,
        residual,
        ff_in,
        gate_proj,
        up_proj,
        hidden,
        ff_out,
    ) = kept_state
    d_ff_out, grad_post_ff = pullback(rms_scale, ff_out, norm_gain[3], grad_out)
    d_ff_out = d_ff_out.astype(jnp.bfloat16)
    grad_down = outer_dot(hidden, d_ff_out).astype(jnp.bfloat16)
    d_hidden = dot_transposed(d_ff_out, down_weight).astype(jnp.bfloat16)
    d_gate, d_up = pullback(geglu, gate_proj, up_proj, d_hidden.astype(jnp.float32))
    d_gate_up = jnp.concatenate([d_gate.astype(jnp.bfloat16), d_up.astype(jnp.bfloat16)], axis=1)
    grad_gate_up = outer_dot(ff_in, d_gate_up).astype(jnp.bfloat16)
    d_ff_in = dot_transposed(d_gate_up, gu_weight)
    d_resid_part, grad_pre_ff = pullback(rms_scale, residual, norm_gain[2], d_ff_in)
    d_residual = grad_out + d_resid_part
    return (d_residual, (grad_gate_up, grad_down), (grad_pre_ff, grad_post_ff))


def attn_backward(d_residual, kept_state, params, layout):
    qkv_weight, out_weight, gu_weight, down_weight, norm_gain, head_gain = params
    unused_own, unused_prior, cosine, sine_table = layout
    (
        inputs,
        normed_in,
        query_proj,
        key_proj,
        query_heads,
        key_rot,
        value_proj,
        prior_keys,
        prior_values,
        probs_own,
        probs_prior,
        mixed,
        attn_proj,
        residual,
        ff_in,
        gate_proj,
        up_proj,
        hidden,
        ff_out,
    ) = kept_state
    row_count = inputs.shape[0]
    head_size = head_gain.shape[1]
    query_width = out_weight.shape[0]
    head_count = query_width // head_size
    scale_factor = head_size ** (-0.5)
    d_attn, grad_post_attn = pullback(rms_scale, attn_proj, norm_gain[1], d_residual)
    d_attn = d_attn.astype(jnp.bfloat16)
    grad_out_proj = outer_dot(mixed, d_attn).astype(jnp.bfloat16)
    d_mixed = dot_transposed(d_attn, out_weight).astype(jnp.bfloat16)
    d_mixed_heads = d_mixed.reshape(row_count, head_count, head_size).transpose(1, 0, 2)
    dot_terms = d_mixed.astype(jnp.float32) * mixed.astype(jnp.float32)
    row_dots = jnp.stack(
        [
            jnp.sum(dot_terms[:, h * head_size : (h + 1) * head_size], axis=-1, keepdims=True)
            for h in range(head_count)
        ]
    )

    def against(keys, values, probs):
        d_values = jnp.einsum(
            "hqk,hqd->kd", probs, d_mixed_heads, preferred_element_type=jnp.float32
        )
        d_probs = jnp.einsum(
            "hqd,kd->hqk", d_mixed_heads, values, preferred_element_type=jnp.float32
        )
        d_scores = (probs.astype(jnp.float32) * (d_probs - row_dots)).astype(jnp.bfloat16)
        d_keys = (
            jnp.einsum("hqk,hqd->kd", d_scores, query_heads, preferred_element_type=jnp.float32)
            * scale_factor
        )
        return (d_keys, d_values, d_scores)

    d_prior_keys, d_prior_values, d_prior_scores = against(prior_keys, prior_values, probs_prior)
    returned = from_behind(
        jnp.concatenate([d_prior_keys, d_prior_values], axis=1).astype(jnp.bfloat16), "fsdp", -1
    ).astype(jnp.float32)
    d_own_keys, d_own_values, d_own_scores = against(key_rot, value_proj, probs_own)
    d_query_heads = (
        jnp.einsum("hqk,kd->hqd", d_own_scores, key_rot, preferred_element_type=jnp.float32)
        + jnp.einsum("hqk,kd->hqd", d_prior_scores, prior_keys, preferred_element_type=jnp.float32)
    ) * scale_factor
    d_query_rows = d_query_heads.transpose(1, 0, 2)
    d_key_rot = d_own_keys + returned[:, :head_size]
    d_value = (d_own_values + returned[:, head_size:]).astype(jnp.bfloat16)

    def query_head(vector, gain_vec):
        return rotate(rms_scale(vector, gain_vec), cosine[:, None, :], sine_table[:, None, :])

    def key_head(vector, gain_vec):
        return rotate(rms_scale(vector, gain_vec), cosine, sine_table)

    d_query, grad_query_gain = pullback(query_head, query_proj, head_gain[0], d_query_rows)
    d_key, grad_key_gain = pullback(key_head, key_proj, head_gain[1], d_key_rot)
    d_query = d_query.reshape(row_count, query_width).astype(jnp.bfloat16)
    d_qkv = jnp.concatenate([d_query, d_key.astype(jnp.bfloat16), d_value], axis=1)
    grad_qkv = outer_dot(normed_in, d_qkv).astype(jnp.bfloat16)
    d_normed = dot_transposed(d_qkv, qkv_weight)
    d_input_part, grad_in_gain = pullback(rms_scale, inputs, norm_gain[0], d_normed)
    d_inputs = d_residual + d_input_part
    gain_grads = (grad_in_gain, grad_post_attn, grad_query_gain, grad_key_gain)
    return (d_inputs, (grad_qkv, grad_out_proj), gain_grads)


def with_gains(blocks, attn_gains, ff_gains):
    size = blocks.shape[0]
    norm_part = jnp.stack([attn_gains[0], attn_gains[1], ff_gains[0], ff_gains[1]])
    norm_part = norm_part.reshape(4, size, -1).transpose(1, 0, 2).reshape(size, -1)
    head_part = jnp.stack(attn_gains[2:]).reshape(2, size, -1).transpose(1, 0, 2).reshape(size, -1)
    row = jnp.concatenate([norm_part, head_part], axis=1).astype(blocks.dtype)
    row = jnp.pad(row[:, None, None], ((0, 0), (0, 0), (0, 15), (0, blocks.shape[3] - row.shape[1])))
    return jnp.concatenate([blocks, jnp.broadcast_to(row, (size, 2) + row.shape[2:])], axis=2)


def local(
    tokens,
    cotangent,
    lengths,
    query_weight,
    key_weight,
    value_weight,
    out_weight,
    gate_weight,
    up_weight,
    down_weight,
    norm_gains,
    head_gains,
):
    core = lax.axis_index("section")
    me = lax.axis_index("fsdp")
    first_core = core == 0
    row_count = tokens.shape[2]
    width = tokens.shape[3]
    query_width = query_weight.shape[2]
    head_size = key_weight.shape[2]
    qkv_width = query_width + 2 * head_size
    ff_width = gate_weight.shape[2]
    out_rows = out_weight.shape[1] // 2

    gain_count, gain_share = norm_gains.shape[1:]
    head_share = head_gains.shape[2]
    split_at = gain_count * gain_share
    gain_rows = jnp.stack(
        [
            norm_gains.reshape(split_at),
            jnp.pad(head_gains.reshape(-1), (0, split_at - 2 * head_share)),
        ]
    )
    gain_rows = jnp.pad(gain_rows, ((0, 14), (0, 0)))

    wide = jnp.concatenate(
        [query_weight[0], key_weight[0], value_weight[0], gate_weight[0], up_weight[0]], axis=1
    )
    wide = wide.reshape(2, -1, wide.shape[1])
    narrow = jnp.concatenate(
        [
            out_weight[0].reshape(2, -1, width),
            down_weight[0].reshape(2, -1, width),
            jnp.broadcast_to(gain_rows[None], (2,) + gain_rows.shape),
        ],
        axis=1,
    )
    layer_blocks = []
    for packed in (wide, narrow):
        arrived = swap_cores(lax.dynamic_index_in_dim(packed, 1 - core, 0, keepdims=False))
        kept = lax.dynamic_index_in_dim(packed, core, 0, keepdims=False)
        layer_blocks.append(
            (jnp.where(first_core, kept, arrived), jnp.where(first_core, arrived, kept))
        )

    def assemble(near_pair):
        wide_held, narrow_held = (gather_rows(pieces) for pieces in near_pair)
        wide_pair = (wide_held, swap_cores(wide_held))
        narrow_pair = (narrow_held, swap_cores(narrow_held))
        everything = slice(None)
        narrow_out = tuple(piece[:, :out_rows] for piece in narrow_pair)
        narrow_down = tuple(
            piece[:, out_rows : piece.shape[1] - gain_rows.shape[0]] for piece in narrow_pair
        )
        held_gains = narrow_held[:, narrow_held.shape[1] - gain_rows.shape[0] :]
        size = held_gains.shape[0]
        norm_gain = held_gains[:, 0].reshape(size, gain_count, gain_share)
        head_gain = held_gains[:, 1, : 2 * head_share].reshape(size, 2, head_share)
        return (
            join_rows(wide_pair, slice(0, qkv_width)),
            join_rows(narrow_out, everything),
            join_rows(wide_pair, slice(qkv_width, None)),
            join_rows(narrow_down, everything),
            norm_gain.transpose(1, 0, 2).reshape(gain_count, -1).astype(jnp.float32),
            head_gain.transpose(1, 0, 2).reshape(2, -1).astype(jnp.float32),
        )

    lower_near = [near_rows(blocks[0]) for blocks in layer_blocks]
    lower_near, upper_blocks = lax.optimization_barrier(
        (lower_near, [blocks[1] for blocks in layer_blocks])
    )
    upper_near = [near_rows(block) for block in upper_blocks]
    lower_params = assemble(lower_near)

    def own_micro(rows):
        return lax.dynamic_index_in_dim(rows, core, 0, keepdims=False)[0]

    doc_lengths = own_micro(lengths)
    places = me * row_count + jnp.arange(row_count, dtype=jnp.int32)
    prior_places = places - row_count
    doc_ids, offset = doc_layout(doc_lengths, places)
    prior_docs, unused = doc_layout(doc_lengths, prior_places)
    layout = (
        window_mask(doc_ids, places, doc_ids, places),
        window_mask(doc_ids, places, prior_docs, prior_places),
    ) + angle_tables(offset, head_size)

    lower_out, lower_state, upper_near = layer_forward(
        own_micro(tokens).astype(jnp.float32), lower_params, layout, upper_near
    )
    upper_params = assemble(upper_near)
    lower_out = lower_out.astype(jnp.bfloat16)
    upper_out, upper_state, unused = layer_forward(
        lower_out.astype(jnp.float32), upper_params, layout, ()
    )
    upper_out = upper_out.astype(jnp.bfloat16)

    d_residual, upper_ff, upper_ff_gains = ff_backward(
        own_micro(cotangent).astype(jnp.float32), upper_state, upper_params
    )
    upper_ff = [add_near(add_cores(row_blocks(grad))) for grad in upper_ff]
    d_middle, upper_attn, upper_attn_gains = attn_backward(
        d_residual, upper_state, upper_params, layout
    )
    upper_attn = [
        with_gains(row_blocks(upper_attn[0]), upper_attn_gains, upper_ff_gains),
        row_blocks(upper_attn[1]),
    ]
    d_middle, upper_ff = lax.optimization_barrier((d_middle, upper_ff))
    upper_ff = [add_far(pair) for pair in upper_ff]
    upper_attn = [add_near(add_cores(blocks)) for blocks in upper_attn]
    d_residual, lower_ff, lower_ff_gains = ff_backward(
        d_middle.astype(jnp.bfloat16).astype(jnp.float32), lower_state, lower_params
    )
    d_residual, upper_ff, upper_attn = lax.optimization_barrier(
        (d_residual, upper_ff, upper_attn)
    )
    upper_ff = [lax.psum(total, "rep") for total in upper_ff]
    upper_attn = [add_far(pair) for pair in upper_attn]
    lower_ff = [add_near(add_cores(row_blocks(grad))) for grad in lower_ff]
    d_tokens, lower_attn, lower_attn_gains = attn_backward(
        d_residual, lower_state, lower_params, layout
    )
    lower_attn = [
        with_gains(row_blocks(lower_attn[0]), lower_attn_gains, lower_ff_gains),
        row_blocks(lower_attn[1]),
    ]
    d_tokens, lower_attn, lower_ff, upper_attn = lax.optimization_barrier(
        (d_tokens, lower_attn, lower_ff, upper_attn)
    )
    lower_ff = [add_far(pair) for pair in lower_ff]
    upper_ff, rest = lax.optimization_barrier((upper_ff, upper_attn + lower_ff))
    rest = [lax.psum(total, "rep") for total in rest]
    lower_attn = [add_far(add_near(add_cores(blocks))) for blocks in lower_attn]
    rest, lower_attn = lax.optimization_barrier((rest, lower_attn))
    lower_attn = [lax.psum(total, "rep") for total in lower_attn]
    upper_sums = rest[:2] + upper_ff
    lower_sums = lower_attn + rest[2:]

    def for_layers(lower_value, upper_value):
        mine = jnp.where(first_core, lower_value, upper_value)
        theirs = jnp.where(first_core, upper_value, lower_value)
        return (mine, swap_cores(theirs.astype(jnp.bfloat16)).astype(mine.dtype))

    section_out = ordered(*(rows[None] for rows in for_layers(lower_out, upper_out)), 0)
    input_grad = ordered(*(rows[None] for rows in for_layers(d_tokens, d_middle)), 0)
    pairs = [
        for_layers(lower_sum, upper_sum) for lower_sum, upper_sum in zip(lower_sums, upper_sums)
    ]
    gain_sums = pairs[0][0][-16].astype(jnp.float32)
    norm_sums = gain_sums[:split_at].reshape(1, gain_count, gain_share)
    head_sums = gain_sums[split_at : split_at + 2 * head_share].reshape(1, 2, head_share)
    pairs[0] = tuple(piece[:-16] for piece in pairs[0])
    shares = [ordered(*pair, 0).astype(jnp.float32)[None] for pair in pairs]
    qkv_share, out_share, gate_up_share, down_share = shares
    return (
        section_out[None, :, None],
        input_grad[None, :, None],
        qkv_share[:, :, :query_width],
        qkv_share[:, :, query_width : query_width + head_size],
        qkv_share[:, :, query_width + head_size :],
        out_share,
        gate_up_share[:, :, :ff_width],
        gate_up_share[:, :, ff_width:],
        down_share,
        norm_sums,
        head_sums,
    )


def solution(mesh):
    return jax.shard_map(
        local,
        mesh=mesh,
        in_specs=(
            P(None, "rep", "fsdp", None),
            P(None, "rep", "fsdp", None),
            P(None, "rep", None),
            P("section", "fsdp", None),
            P("section", "fsdp", None),
            P("section", "fsdp", None),
            P("section", "fsdp", None),
            P("section", "fsdp", None),
            P("section", "fsdp", None),
            P("section", "fsdp", None),
            P("section", None, "fsdp"),
            P("section", None, "fsdp"),
        ),
        out_specs=(
            P("section", None, "rep", "fsdp", None),
            P("section", None, "rep", "fsdp", None),
            P("section", "fsdp", None),
            P("section", "fsdp", None),
            P("section", "fsdp", None),
            P("section", "fsdp", None),
            P("section", "fsdp", None),
            P("section", "fsdp", None),
            P("section", "fsdp", None),
            P("section", None, "fsdp"),
            P("section", None, "fsdp"),
        ),
        check_vma=False,
    )
```

profile of v0, /device:TPU:0, one launch (start us, length us, event | category | flops | bytes accessed | tf_op | source)
XLA Modules:
  0.0 597.8 jit_solution(17354293956497261510)
XLA Ops:
  14.2 2.5 bitcast_select_fusion
  16.7 2.8 collective-permute-start.1
  23.5 27.0 %collective-permute-done.4 = bf16[400,640]{1,0:T(8,128)(2,1)} collective-permute-done((bf16[400,640]{1,0:T(8,128)(2,1)S(1)}, bf16[400,640]{1,0:T(8,128)(2,1)}, u32[]{:S(2)}, u32[]{:S(2)}) %collective-permute-start.4) | collective-permute-done | bytes 512032 | tf_op jit(solution)/shard_map/ppermute | solution.py:115
  54.1 2.1 broadcast.590.clone
  57.2 2.2 bitcast_dynamic-update-slice_fusion.6
  60.4 9.5 %collective-permute-done.7 = bf16[80,5632]{1,0:T(8,128)(2,1)S(1)} collective-permute-done((bf16[80,5632]{1,0:T(8,128)(2,1)}, bf16[80,5632]{1,0:T(8,128)(2,1)S(1)}, u32[]{:S(2)}, u32[]{:S(2)}) %collective-permute-start.7) | collective-permute-done | bytes 901152 | tf_op jit(solution)/shard_map/ppermute | solution.py:115
  74.6 2.2 collective-permute-start.11
  93.3 2.7 copy.149
  95.9 2.7 multiply_reduce_fusion.5
  100.7 4.2 collective-permute-start.9
  104.9 2.9 select_bitcast_fusion.3
  110.5 9.0 %collective-permute-done.9 = bf16[512,512]{0,1:T(8,128)(2,1)S(1)} collective-permute-done((bf16[512,512]{0,1:T(8,128)(2,1)S(1)}, bf16[512,512]{0,1:T(8,128)(2,1)S(1)}, u32[]{:S(2)}, u32[]{:S(2)}) %collective-permute-start.9) | collective-permute-done | bytes 524320 | tf_op jit(solution)/shard_map/ppermute | solution.py:20
  122.3 2.0 multiply_convert_fusion.8
  133.7 2.0 broadcast.590
  135.8 2.2 bitcast_dynamic-update-slice_fusion.3
  138.0 2.2 bitcast_dynamic-update-slice_fusion.2
  141.4 2.2 bitcast_dynamic-update-slice_fusion.1
  145.6 3.4 collective-permute-done.16
  150.7 4.3 multiply_convert_fusion.7
  155.0 2.4 copy.194
  157.4 4.2 multiply_reduce_fusion.17
  175.1 3.1 select_bitcast_fusion.1
  181.4 4.4 collective-permute-start.18
  188.7 8.5 %collective-permute-done.18 = bf16[512,512]{0,1:T(8,128)(2,1)S(1)} collective-permute-done((bf16[512,512]{0,1:T(8,128)(2,1)S(1)}, bf16[512,512]{0,1:T(8,128)(2,1)S(1)}, u32[]{:S(2)}, u32[]{:S(2)}) %collective-permute-start.18) | collective-permute-done | bytes 524320 | tf_op jit(solution)/shard_map/ppermute | solution.py:20
  198.1 2.1 fusion.21
  200.2 2.0 multiply_convert_fusion.5
  208.8 3.9 multiply_convert_fusion.4
  215.9 8.3 %fusion.9 = (bf16[512,2048]{1,0:T(8,128)(2,1)S(1)}, bf16[512,2048]{1,0:T(8,128)(2,1)S(1)}) fusion(f32[512,2048]{1,0:T(8,128)} %copy-done.203, f32[512,2048]{1,0:T(8,128)} %get-tuple-element.321, bf16[2048,640]{1,0:T(8,128)(2,1)S(1)} %bitcast.529, f32[512,640]{1,0:T(8,128)S(1)} %get-tuple-element.323, f32[512]{0:T(512)S(1)} %multiply_multiply_fusion.19, ...), kind=kOutput, calls=%fused_computation.27 | convolution fusion | flops 1375928320 | bytes 17178628 | tf_op jit(solution)/shard_map/dot_general | solution.py:84
  224.3 4.0 multiply_reduce_fusion.9
  230.0 2.1 convolution_convert_fusion.9
  234.0 2.3 copy.173
  236.3 5.8 convolution_convert_fusion.3
  242.2 4.9 convolution_convert_fusion.1
  249.4 2.4 copy.255
  267.7 2.1 multiply_reduce_fusion.2
  269.8 2.5 dynamic-slice_bitcast_fusion.3
  272.8 3.7 dynamic-slice_bitcast_fusion.1
  277.7 5.7 collective-permute-done.21
  289.1 2.7 convolution_convert_fusion.5
  291.8 2.6 fusion.48
  299.6 2.7 collective-permute-start.31
  307.3 2.7 convert_add_fusion.1
  317.3 19.2 %collective-permute-done.29 = bf16[2,96,1536]{2,1,0:T(8,128)(2,1)S(1)} collective-permute-done((bf16[2,96,1536]{2,1,0:T(8,128)(2,1)S(1)}, bf16[2,96,1536]{2,1,0:T(8,128)(2,1)S(1)}, u32[]{:S(2)}, u32[]{:S(2)}) %collective-permute-start.29) | collective-permute-done | bytes 589856 | tf_op jit(solution)/shard_map/ppermute | solution.py:115
  342.0 2.0 convolution_convert_fusion.2
  345.0 6.7 %fusion.5 = (bf16[512,2048]{1,0:T(8,128)(2,1)S(1)}, bf16[512,2048]{1,0:T(8,128)(2,1)S(1)}) fusion(f32[512,2048]{1,0:T(8,128)S(1)} %copy-done.202, f32[512,2048]{1,0:T(8,128)S(1)} %copy-done.207, bf16[2048,640]{1,0:T(8,128)(2,1)S(1)} %bitcast.527, bf16[512,640]{1,0:T(8,128)(2,1)S(1)} %get-tuple-element.198, f32[512,640]{1,0:T(8,128)S(1)} %copy-done.57, ...), kind=kOutput, calls=%fused_computation.23 | convolution fusion | flops 1375928320 | bytes 17177088 | tf_op jit(solution)/shard_map/dot_general | solution.py:84
  351.7 4.5 multiply_reduce_fusion.6
  356.3 3.3 convolution_convert_fusion
  369.0 5.1 collective-permute-done.26
  374.0 2.1 add_convert_fusion.3
  377.7 2.1 convolution_convert_fusion.8
  403.9 7.4 %collective-permute-done.32 = bf16[512,512]{0,1:T(8,128)(2,1)} collective-permute-done((bf16[512,512]{0,1:T(8,128)(2,1)}, bf16[512,512]{0,1:T(8,128)(2,1)}, u32[]{:S(2)}, u32[]{:S(2)}) %collective-permute-start.32) | collective-permute-done | bytes 524320 | tf_op jit(solution)/shard_map/ppermute | solution.py:20
  417.6 2.6 fusion.52
  420.7 3.0 convolution_convert_fusion.4
  427.1 2.7 convert_add_fusion
  430.0 2.6 collective-permute-start.34
  433.2 22.1 %collective-permute-done.36 = bf16[2,256,640]{2,1,0:T(8,128)(2,1)S(1)} collective-permute-done((bf16[2,256,640]{2,1,0:T(8,128)(2,1)S(1)}, bf16[2,256,640]{2,1,0:T(8,128)(2,1)S(1)}, u32[]{:S(2)}, u32[]{:S(2)}) %collective-permute-start.36) | collective-permute-done | bytes 655392 | tf_op jit(solution)/shard_map/ppermute | solution.py:115
  461.6 2.7 collective-permute-done.41
  467.2 2.0 collective-permute-start.46
  469.2 3.7 collective-permute-done.40
  476.3 2.4 collective-permute-start.43
  480.0 7.0 %collective-permute-done.43 = bf16[2,96,1536]{2,1,0:T(8,128)(2,1)S(1)} collective-permute-done((bf16[2,96,1536]{2,1,0:T(8,128)(2,1)S(1)}, bf16[2,96,1536]{2,1,0:T(8,128)(2,1)S(1)}, u32[]{:S(2)}, u32[]{:S(2)}) %collective-permute-start.43) | collective-permute-done | bytes 589856 | tf_op jit(solution)/shard_map/ppermute | solution.py:115
  491.6 2.5 collective-permute-done.44
  494.9 46.2 %all-reduce.21.cloned.1.call-done = (bf16[96,1536]{1,0:T(8,128)(2,1)}, bf16[128,640]{1,0:T(8,128)(2,1)}, bf16[80,4096]{1,0:T(8,128)(2,1)}, bf16[256,640]{1,0:T(8,128)(2,1)}) async-done(((bf16[96,1536]{1,0:T(8,128)(2,1)}, bf16[128,640]{1,0:T(8,128)(2,1)}, bf16[80,4096]{1,0:T(8,128)(2,1)}, bf16[256,640]{1,0:T(8,128)(2,1)}), (bf16[96,1536]{1,0:T(8,128)(2,1)}, bf16[128,640]{1,0:T(8,128)(2,1)}, ...) | async-done | bytes 1441808 | tf_op jit(solution)/shard_map/psum | solution.py:540
  545.2 36.0 %all-reduce.19.cloned.1.call-done = (bf16[96,1536]{1,0:T(8,128)(2,1)}, bf16[128,640]{1,0:T(8,128)(2,1)}) async-done(((bf16[96,1536]{1,0:T(8,128)(2,1)}, bf16[128,640]{1,0:T(8,128)(2,1)}), (bf16[96,1536]{1,0:T(8,128)(2,1)}, bf16[128,640]{1,0:T(8,128)(2,1)})) %all-reduce.19.cloned.1.call-update) | async-done | bytes 458768 | tf_op jit(solution)/shard_map/psum | solution.py:543
  (828 shorter events, 219.2 us)
Async XLA Ops:
  7.2 466.7 %all-reduce.23.cloned.1.call-start = ((), (), s32[]{:S(2)}) async-start(), calls=%async_computation.2 | async-start | bytes 1966080 | tf_op jit(solution)/shard_map/psum | solution.py:525
  11.5 2.8 collective-permute-start
  13.7 7.3 %collective-permute-start.3 = (bf16[400,640]{1,0:T(8,128)(2,1)S(1)}, bf16[400,640]{1,0:T(8,128)(2,1)}, u32[]{:S(2)}, u32[]{:S(2)}) collective-permute-start(bf16[400,640]{1,0:T(8,128)(2,1)S(1)} %dynamic-slice_bitcast_fusion.8), channel_id=1, source_target_pairs={{0,16},{16,0},{1,17},{17,1},{2,18},{18,2},{3,19},{19,3},{4,20},{20... | collective-permute-start | bytes 1536008 | tf_op jit(solution)/shard_map/ppermute | solution.py:119
  16.7 34.2 %collective-permute-start.1 = (bf16[80,5632]{1,0:T(8,128)(2,1)S(1)}, bf16[80,5632]{1,0:T(8,128)(2,1)}, u32[]{:S(2)}, u32[]{:S(2)}) collective-permute-start(bf16[80,5632]{1,0:T(8,128)(2,1)S(1)} %get-tuple-element.62), channel_id=1, source_target_pairs={{0,4},{4,0},{8,12},{12,8},{16,24},{20,28},{24,16},{28,20},{1,5},{5... | collective-permute-start | bytes 2703368 | tf_op jit(solution)/shard_map/ppermute | solution.py:115
  19.5 31.4 %collective-permute-start.2 = (bf16[80,5632]{1,0:T(8,128)(2,1)S(1)}, bf16[80,5632]{1,0:T(8,128)(2,1)S(1)}, u32[]{:S(2)}, u32[]{:S(2)}) collective-permute-start(bf16[80,5632]{1,0:T(8,128)(2,1)S(1)} %get-tuple-element.62), channel_id=1, source_target_pairs={{0,8},{4,12},{8,0},{12,4},{16,20},{20,16},{24,28},{28,24},{1,9},{5... | collective-permute-start | bytes 2703368 | tf_op jit(solution)/shard_map/ppermute | solution.py:115
  23.0 27.5 %collective-permute-start.4 = (bf16[400,640]{1,0:T(8,128)(2,1)S(1)}, bf16[400,640]{1,0:T(8,128)(2,1)}, u32[]{:S(2)}, u32[]{:S(2)}) collective-permute-start(bf16[400,640]{1,0:T(8,128)(2,1)S(1)} %get-tuple-element.59), channel_id=1, source_target_pairs={{0,4},{4,0},{8,12},{12,8},{16,24},{20,28},{24,16},{28,20},{1,5},{5... | collective-permute-start | bytes 1536008 | tf_op jit(solution)/shard_map/ppermute | solution.py:115
  23.5 27.4 %collective-permute-start.5 = (bf16[400,640]{1,0:T(8,128)(2,1)S(1)}, bf16[400,640]{1,0:T(8,128)(2,1)S(1)}, u32[]{:S(2)}, u32[]{:S(2)}) collective-permute-start(bf16[400,640]{1,0:T(8,128)(2,1)S(1)} %get-tuple-element.59), channel_id=1, source_target_pairs={{0,8},{4,12},{8,0},{12,4},{16,20},{20,16},{24,28},{28,24},{1,9},{5... | collective-permute-start | bytes 1536008 | tf_op jit(solution)/shard_map/ppermute | solution.py:115
  50.9 21.2 %collective-permute-start.6 = (bf16[400,640]{1,0:T(8,128)(2,1)}, bf16[400,640]{1,0:T(8,128)(2,1)S(1)}, u32[]{:S(2)}, u32[]{:S(2)}) collective-permute-start(bf16[400,640]{1,0:T(8,128)(2,1)} %collective-permute-done.4), channel_id=1, source_target_pairs={{0,8},{4,12},{8,0},{12,4},{16,20},{20,16},{24,28},{28,24},{1,9},{5... | collective-permute-start | bytes 1536008 | tf_op jit(solution)/shard_map/ppermute | solution.py:115
  52.8 17.0 %collective-permute-start.7 = (bf16[80,5632]{1,0:T(8,128)(2,1)}, bf16[80,5632]{1,0:T(8,128)(2,1)S(1)}, u32[]{:S(2)}, u32[]{:S(2)}) collective-permute-start(bf16[80,5632]{1,0:T(8,128)(2,1)} %collective-permute-done.1), channel_id=1, source_target_pairs={{0,8},{4,12},{8,0},{12,4},{16,20},{20,16},{24,28},{28,24},{1,9},{5... | collective-permute-start | bytes 2703368 | tf_op jit(solution)/shard_map/ppermute | solution.py:115
  70.9 17.2 %collective-permute-start.8 = (bf16[4,80,5632]{2,1,0:T(8,128)(2,1)}, bf16[4,80,5632]{2,1,0:T(8,128)(2,1)}, u32[]{:S(2)}, u32[]{:S(2)}) collective-permute-start(bf16[4,80,5632]{2,1,0:T(8,128)(2,1)} %bitcast_dynamic-update-slice_fusion.4), channel_id=1, source_target_pairs={{0,16},{16,0},{1,17},{17,1},{2,18},{18,2},{3,19},{19,3},{4,20},{20... | collective-permute-start | bytes 10813448 | tf_op jit(solution)/shard_map/ppermute | solution.py:119
  72.2 8.1 %collective-permute-start.10 = (bf16[4,400,640]{2,1,0:T(8,128)(2,1)S(1)}, bf16[4,400,640]{2,1,0:T(8,128)(2,1)}, u32[]{:S(2)}, u32[]{:S(2)}) collective-permute-start(bf16[4,400,640]{2,1,0:T(8,128)(2,1)S(1)} %bitcast_dynamic-update-slice_fusion.12), channel_id=1, source_target_pairs={{0,16},{16,0},{1,17},{17,1},{2,18},{18,2},{3,19},{19,3},{4,20},{20... | collective-permute-start | bytes 6144008 | tf_op jit(solution)/shard_map/ppermute | solution.py:119
  74.5 47.7 %copy-start.48 = (pred[512,512]{0,1:T(8,128)(4,1)}, pred[512,512]{0,1:T(8,128)(4,1)S(1)}, u32[]{:S(2)}) copy-start(pred[512,512]{0,1:T(8,128)(4,1)S(1)} %get-tuple-element.294) | copy-start | bytes 786436
  74.5 47.7 %copy-start.50 = (pred[512,512]{0,1:T(8,128)(4,1)}, pred[512,512]{0,1:T(8,128)(4,1)S(1)}, u32[]{:S(2)}) copy-start(pred[512,512]{0,1:T(8,128)(4,1)S(1)} %get-tuple-element.295) | copy-start | bytes 786436
  74.6 55.5 %collective-permute-start.11 = (bf16[80,5632]{1,0:T(8,128)(2,1)}, bf16[80,5632]{1,0:T(8,128)(2,1)}, u32[]{:S(2)}, u32[]{:S(2)}) collective-permute-start(bf16[80,5632]{1,0:T(8,128)(2,1)} %get-tuple-element.71), channel_id=1, source_target_pairs={{0,4},{4,0},{8,12},{12,8},{16,24},{20,28},{24,16},{28,20},{1,5},{5... | collective-permute-start | bytes 2703368 | tf_op jit(solution)/shard_map/ppermute | solution.py:115
  76.8 53.2 %collective-permute-start.12 = (bf16[80,5632]{1,0:T(8,128)(2,1)}, bf16[80,5632]{1,0:T(8,128)(2,1)}, u32[]{:S(2)}, u32[]{:S(2)}) collective-permute-start(bf16[80,5632]{1,0:T(8,128)(2,1)} %get-tuple-element.71), channel_id=1, source_target_pairs={{0,8},{4,12},{8,0},{12,4},{16,20},{20,16},{24,28},{28,24},{1,9},{5... | collective-permute-start | bytes 2703368 | tf_op jit(solution)/shard_map/ppermute | solution.py:115
  78.1 51.9 %collective-permute-start.13 = (bf16[400,640]{1,0:T(8,128)(2,1)}, bf16[400,640]{1,0:T(8,128)(2,1)}, u32[]{:S(2)}, u32[]{:S(2)}) collective-permute-start(bf16[400,640]{1,0:T(8,128)(2,1)} %get-tuple-element.68), channel_id=1, source_target_pairs={{0,4},{4,0},{8,12},{12,8},{16,24},{20,28},{24,16},{28,20},{1,5},{5... | collective-permute-start | bytes 1536008 | tf_op jit(solution)/shard_map/ppermute | solution.py:115
  79.1 49.6 %copy-start.132 = (f32[640]{0:T(1024)}, f32[640]{0:T(1024)S(1)}, u32[]{:S(2)}) copy-start(f32[640]{0:T(1024)S(1)} %mul.1173) | copy-start | bytes 7684
  79.2 64.4 %copy-start.134 = (f32[640]{0:T(1024)}, f32[640]{0:T(1024)S(1)}, u32[]{:S(2)}) copy-start(f32[640]{0:T(1024)S(1)} %mul.1179) | copy-start | bytes 7684
  79.3 83.0 %copy-start.136 = (f32[640]{0:T(1024)}, f32[640]{0:T(1024)S(1)}, u32[]{:S(2)}) copy-start(f32[640]{0:T(1024)S(1)} %mul.1192) | copy-start | bytes 7684
  80.3 49.7 %collective-permute-start.14 = (bf16[400,640]{1,0:T(8,128)(2,1)}, bf16[400,640]{1,0:T(8,128)(2,1)}, u32[]{:S(2)}, u32[]{:S(2)}) collective-permute-start(bf16[400,640]{1,0:T(8,128)(2,1)} %get-tuple-element.68), channel_id=1, source_target_pairs={{0,8},{4,12},{8,0},{12,4},{16,20},{20,16},{24,28},{28,24},{1,9},{5... | collective-permute-start | bytes 1536008 | tf_op jit(solution)/shard_map/ppermute | solution.py:115
  100.7 18.8 %collective-permute-start.9 = (bf16[512,512]{0,1:T(8,128)(2,1)S(1)}, bf16[512,512]{0,1:T(8,128)(2,1)S(1)}, u32[]{:S(2)}, u32[]{:S(2)}) collective-permute-start(bf16[512,512]{0,1:T(8,128)(2,1)S(1)} %pad_maximum_fusion.28), channel_id=1, source_target_pairs={{0,4},{4,8},{8,12},{1,5},{5,9},{9,13},{2,6},{6,10},{10,14},{3,7},{... | collective-permute-start | bytes 1572872 | tf_op jit(solution)/shard_map/ppermute | solution.py:20
  108.9 41.8 %copy-start.58 = (bf16[4,2,80,4096]{3,2,1,0:T(8,128)(2,1)}, bf16[4,2,80,4096]{3,2,1,0:T(8,128)(2,1)S(1)}, u32[]{:S(2)}) copy-start(bf16[4,2,80,4096]{3,2,1,0:T(8,128)(2,1)S(1)} %copy.157) | copy-start | bytes 15728644
  130.1 20.0 %collective-permute-start.15 = (bf16[400,640]{1,0:T(8,128)(2,1)}, bf16[400,640]{1,0:T(8,128)(2,1)S(1)}, u32[]{:S(2)}, u32[]{:S(2)}) collective-permute-start(bf16[400,640]{1,0:T(8,128)(2,1)} %collective-permute-done.13), channel_id=1, source_target_pairs={{0,8},{4,12},{8,0},{12,4},{16,20},{20,16},{24,28},{28,24},{1,9},{5... | collective-permute-start | bytes 1536008 | tf_op jit(solution)/shard_map/ppermute | solution.py:115
  133.2 15.8 %collective-permute-start.16 = (bf16[80,5632]{1,0:T(8,128)(2,1)}, bf16[80,5632]{1,0:T(8,128)(2,1)S(1)}, u32[]{:S(2)}, u32[]{:S(2)}) collective-permute-start(bf16[80,5632]{1,0:T(8,128)(2,1)} %collective-permute-done.11), channel_id=1, source_target_pairs={{0,8},{4,12},{8,0},{12,4},{16,20},{20,16},{24,28},{28,24},{1,9},{5... | collective-permute-start | bytes 2703368 | tf_op jit(solution)/shard_map/ppermute | solution.py:115
  150.0 20.2 %collective-permute-start.17 = (bf16[4,80,5632]{2,1,0:T(8,128)(2,1)}, bf16[4,80,5632]{2,1,0:T(8,128)(2,1)}, u32[]{:S(2)}, u32[]{:S(2)}) collective-permute-start(bf16[4,80,5632]{2,1,0:T(8,128)(2,1)} %bitcast_dynamic-update-slice_fusion), channel_id=1, source_target_pairs={{0,16},{16,0},{1,17},{17,1},{2,18},{18,2},{3,19},{19,3},{4,20},{20... | collective-permute-start | bytes 10813448 | tf_op jit(solution)/shard_map/ppermute | solution.py:119
  150.1 16.5 %collective-permute-start.19 = (bf16[4,400,640]{2,1,0:T(8,128)(2,1)S(1)}, bf16[4,400,640]{2,1,0:T(8,128)(2,1)}, u32[]{:S(2)}, u32[]{:S(2)}) collective-permute-start(bf16[4,400,640]{2,1,0:T(8,128)(2,1)S(1)} %bitcast_dynamic-update-slice_fusion.8), channel_id=1, source_target_pairs={{0,16},{16,0},{1,17},{17,1},{2,18},{18,2},{3,19},{19,3},{4,20},{20... | collective-permute-start | bytes 6144008 | tf_op jit(solution)/shard_map/ppermute | solution.py:119
  181.4 15.8 %collective-permute-start.18 = (bf16[512,512]{0,1:T(8,128)(2,1)S(1)}, bf16[512,512]{0,1:T(8,128)(2,1)S(1)}, u32[]{:S(2)}, u32[]{:S(2)}) collective-permute-start(bf16[512,512]{0,1:T(8,128)(2,1)S(1)} %pad_maximum_fusion.29), channel_id=1, source_target_pairs={{0,4},{4,8},{8,12},{1,5},{5,9},{9,13},{2,6},{6,10},{10,14},{3,7},{... | collective-permute-start | bytes 1572872 | tf_op jit(solution)/shard_map/ppermute | solution.py:20
  249.4 47.9 %collective-permute-start.30 = (bf16[4,128,640]{2,1,0:T(8,128)(2,1)}, bf16[4,128,640]{2,1,0:T(8,128)(2,1)}, u32[]{:S(2)}, u32[]{:S(2)}) collective-permute-start(bf16[4,128,640]{2,1,0:T(8,128)(2,1)} %dynamic-slice_bitcast_fusion.7), channel_id=1, source_target_pairs={{0,16},{16,0},{1,17},{17,1},{2,18},{18,2},{3,19},{19,3},{4,20},{20... | collective-permute-start | bytes 1966088 | tf_op jit(solution)/shard_map/ppermute | solution.py:119
  266.1 17.3 %collective-permute-start.21 = (bf16[512,512]{0,1:T(8,128)(2,1)}, bf16[512,512]{0,1:T(8,128)(2,1)}, u32[]{:S(2)}, u32[]{:S(2)}) collective-permute-start(bf16[512,512]{0,1:T(8,128)(2,1)} %pad_maximum_fusion.30), channel_id=1, source_target_pairs={{4,0},{8,4},{12,8},{5,1},{9,5},{13,9},{6,2},{10,6},{14,10},{7,3},{... | collective-permute-start | bytes 1572872 | tf_op jit(solution)/shard_map/ppermute | solution.py:20
  272.3 31.4 %collective-permute-start.24 = (bf16[4,256,640]{2,1,0:T(8,128)(2,1)}, bf16[4,256,640]{2,1,0:T(8,128)(2,1)}, u32[]{:S(2)}, u32[]{:S(2)}) collective-permute-start(bf16[4,256,640]{2,1,0:T(8,128)(2,1)} %dynamic-slice_bitcast_fusion.3), channel_id=1, source_target_pairs={{0,16},{16,0},{1,17},{17,1},{2,18},{18,2},{3,19},{19,3},{4,20},{20... | collective-permute-start | bytes 3932168 | tf_op jit(solution)/shard_map/ppermute | solution.py:119
  276.5 30.8 %collective-permute-start.22 = (bf16[4,80,4096]{2,1,0:T(8,128)(2,1)}, bf16[4,80,4096]{2,1,0:T(8,128)(2,1)}, u32[]{:S(2)}, u32[]{:S(2)}) collective-permute-start(bf16[4,80,4096]{2,1,0:T(8,128)(2,1)} %dynamic-slice_bitcast_fusion.1), channel_id=1, source_target_pairs={{0,16},{16,0},{1,17},{17,1},{2,18},{18,2},{3,19},{19,3},{4,20},{20... | collective-permute-start | bytes 7864328 | tf_op jit(solution)/shard_map/ppermute | solution.py:119
  276.5 25.8 %collective-permute-start.20 = (bf16[512,640]{1,0:T(8,128)(2,1)}, bf16[512,640]{1,0:T(8,128)(2,1)}, u32[]{:S(2)}, u32[]{:S(2)}) collective-permute-start(bf16[512,640]{1,0:T(8,128)(2,1)} %get-tuple-element.200), channel_id=1, source_target_pairs={{0,16},{16,0},{1,17},{17,1},{2,18},{18,2},{3,19},{19,3},{4,20},{20... | collective-permute-start | bytes 1966088 | tf_op jit(solution)/shard_map/ppermute | solution.py:119
  296.4 9.7 %collective-permute-start.28 = (bf16[4,96,1536]{2,1,0:T(8,128)(2,1)S(1)}, bf16[4,96,1536]{2,1,0:T(8,128)(2,1)S(1)}, u32[]{:S(2)}, u32[]{:S(2)}) collective-permute-start(bf16[4,96,1536]{2,1,0:T(8,128)(2,1)S(1)} %fusion.84), channel_id=1, source_target_pairs={{0,16},{16,0},{1,17},{17,1},{2,18},{18,2},{3,19},{19,3},{4,20},{20... | collective-permute-start | bytes 3538952 | tf_op jit(solution)/shard_map/ppermute | solution.py:119
  297.3 42.4 %copy-start.2 = (f32[512,640]{1,0:T(8,128)}, f32[512,640]{1,0:T(8,128)S(1)}, u32[]{:S(2)}) copy-start(f32[512,640]{1,0:T(8,128)S(1)} %fusion.61) | copy-start | bytes 3932164
  299.6 14.1 %collective-permute-start.31 = (bf16[2,128,640]{2,1,0:T(8,128)(2,1)S(1)}, bf16[2,128,640]{2,1,0:T(8,128)(2,1)S(1)}, u32[]{:S(2)}, u32[]{:S(2)}) collective-permute-start(bf16[2,128,640]{2,1,0:T(8,128)(2,1)S(1)} %pad_maximum_fusion.32), channel_id=1, source_target_pairs={{0,4},{4,0},{8,12},{12,8},{16,24},{20,28},{24,16},{28,20},{1,5},{5... | collective-permute-start | bytes 983048 | tf_op jit(solution)/shard_map/ppermute | solution.py:115
  305.5 10.7 %collective-permute-start.25 = (bf16[2,256,640]{2,1,0:T(8,128)(2,1)S(1)}, bf16[2,256,640]{2,1,0:T(8,128)(2,1)S(1)}, u32[]{:S(2)}, u32[]{:S(2)}) collective-permute-start(bf16[2,256,640]{2,1,0:T(8,128)(2,1)S(1)} %pad_maximum_fusion.20), channel_id=1, source_target_pairs={{0,4},{4,0},{8,12},{12,8},{16,24},{20,28},{24,16},{28,20},{1,5},{5... | collective-permute-start | bytes 1966088 | tf_op jit(solution)/shard_map/ppermute | solution.py:115
  310.3 27.4 %collective-permute-start.23 = (bf16[2,80,4096]{2,1,0:T(8,128)(2,1)S(1)}, bf16[2,80,4096]{2,1,0:T(8,128)(2,1)S(1)}, u32[]{:S(2)}, u32[]{:S(2)}) collective-permute-start(bf16[2,80,4096]{2,1,0:T(8,128)(2,1)S(1)} %pad_maximum_fusion.17), channel_id=1, source_target_pairs={{0,4},{4,0},{8,12},{12,8},{16,24},{20,28},{24,16},{28,20},{1,5},{5... | collective-permute-start | bytes 3932168 | tf_op jit(solution)/shard_map/ppermute | solution.py:115
  311.2 25.4 %collective-permute-start.29 = (bf16[2,96,1536]{2,1,0:T(8,128)(2,1)S(1)}, bf16[2,96,1536]{2,1,0:T(8,128)(2,1)S(1)}, u32[]{:S(2)}, u32[]{:S(2)}) collective-permute-start(bf16[2,96,1536]{2,1,0:T(8,128)(2,1)S(1)} %pad_maximum_fusion.26), channel_id=1, source_target_pairs={{0,4},{4,0},{8,12},{12,8},{16,24},{20,28},{24,16},{28,20},{1,5},{5... | collective-permute-start | bytes 1769480 | tf_op jit(solution)/shard_map/ppermute | solution.py:115
  359.5 7.5 %collective-permute-start.27 = (bf16[256,640]{1,0:T(8,128)(2,1)}, bf16[256,640]{1,0:T(8,128)(2,1)}, u32[]{:S(2)}, u32[]{:S(2)}) collective-permute-start(bf16[256,640]{1,0:T(8,128)(2,1)} %get-tuple-element.78), channel_id=1, source_target_pairs={{0,8},{4,12},{8,0},{12,4},{16,20},{20,16},{24,28},{28,24},{1,9},{5... | collective-permute-start | bytes 983048 | tf_op jit(solution)/shard_map/ppermute | solution.py:115
  359.6 14.4 %collective-permute-start.26 = (bf16[80,4096]{1,0:T(8,128)(2,1)}, bf16[80,4096]{1,0:T(8,128)(2,1)}, u32[]{:S(2)}, u32[]{:S(2)}) collective-permute-start(bf16[80,4096]{1,0:T(8,128)(2,1)} %get-tuple-element.76), channel_id=1, source_target_pairs={{0,8},{4,12},{8,0},{12,4},{16,20},{20,16},{24,28},{28,24},{1,9},{5... | collective-permute-start | bytes 1966088 | tf_op jit(solution)/shard_map/ppermute | solution.py:115
  362.8 61.2 %collective-permute-start.35 = (bf16[4,256,640]{2,1,0:T(8,128)(2,1)}, bf16[4,256,640]{2,1,0:T(8,128)(2,1)}, u32[]{:S(2)}, u32[]{:S(2)}) collective-permute-start(bf16[4,256,640]{2,1,0:T(8,128)(2,1)} %dynamic-slice_bitcast_fusion.2), channel_id=1, source_target_pairs={{0,16},{16,0},{1,17},{17,1},{2,18},{18,2},{3,19},{19,3},{4,20},{20... | collective-permute-start | bytes 3932168 | tf_op jit(solution)/shard_map/ppermute | solution.py:119
  364.5 62.5 %collective-permute-start.33 = (bf16[4,80,4096]{2,1,0:T(8,128)(2,1)}, bf16[4,80,4096]{2,1,0:T(8,128)(2,1)}, u32[]{:S(2)}, u32[]{:S(2)}) collective-permute-start(bf16[4,80,4096]{2,1,0:T(8,128)(2,1)} %dynamic-slice_bitcast_fusion), channel_id=1, source_target_pairs={{0,16},{16,0},{1,17},{17,1},{2,18},{18,2},{3,19},{19,3},{4,20},{20... | collective-permute-start | bytes 7864328 | tf_op jit(solution)/shard_map/ppermute | solution.py:119
  380.8 19.3 %collective-permute-start.38 = (bf16[128,640]{1,0:T(8,128)(2,1)}, bf16[128,640]{1,0:T(8,128)(2,1)}, u32[]{:S(2)}, u32[]{:S(2)}) collective-permute-start(bf16[128,640]{1,0:T(8,128)(2,1)} %get-tuple-element.83), channel_id=1, source_target_pairs={{0,8},{4,12},{8,0},{12,4},{16,20},{20,16},{24,28},{28,24},{1,9},{5... | collective-permute-start | bytes 491528 | tf_op jit(solution)/shard_map/ppermute | solution.py:115
  380.9 21.1 %collective-permute-start.37 = (bf16[96,1536]{1,0:T(8,128)(2,1)}, bf16[96,1536]{1,0:T(8,128)(2,1)}, u32[]{:S(2)}, u32[]{:S(2)}) collective-permute-start(bf16[96,1536]{1,0:T(8,128)(2,1)} %get-tuple-element.81), channel_id=1, source_target_pairs={{0,8},{4,12},{8,0},{12,4},{16,20},{20,16},{24,28},{28,24},{1,9},{5... | collective-permute-start | bytes 884744 | tf_op jit(solution)/shard_map/ppermute | solution.py:115
  398.5 12.8 %collective-permute-start.32 = (bf16[512,512]{0,1:T(8,128)(2,1)}, bf16[512,512]{0,1:T(8,128)(2,1)}, u32[]{:S(2)}, u32[]{:S(2)}) collective-permute-start(bf16[512,512]{0,1:T(8,128)(2,1)} %pad_maximum_fusion.31), channel_id=1, source_target_pairs={{4,0},{8,4},{12,8},{5,1},{9,5},{13,9},{6,2},{10,6},{14,10},{7,3},{... | collective-permute-start | bytes 1572872 | tf_op jit(solution)/shard_map/ppermute | solution.py:20
  400.0 141.1 %all-reduce.21.cloned.1.call-start = ((), (), s32[]{:S(2)}) async-start(), calls=%async_computation.1 | async-start | bytes 2883584 | tf_op jit(solution)/shard_map/psum | solution.py:540
  430.0 25.4 %collective-permute-start.34 = (bf16[2,80,4096]{2,1,0:T(8,128)(2,1)S(1)}, bf16[2,80,4096]{2,1,0:T(8,128)(2,1)S(1)}, u32[]{:S(2)}, u32[]{:S(2)}) collective-permute-start(bf16[2,80,4096]{2,1,0:T(8,128)(2,1)S(1)} %pad_maximum_fusion.18), channel_id=1, source_target_pairs={{0,4},{4,0},{8,12},{12,8},{16,24},{20,28},{24,16},{28,20},{1,5},{5... | collective-permute-start | bytes 3932168 | tf_op jit(solution)/shard_map/ppermute | solution.py:115
  432.8 22.5 %collective-permute-start.36 = (bf16[2,256,640]{2,1,0:T(8,128)(2,1)S(1)}, bf16[2,256,640]{2,1,0:T(8,128)(2,1)S(1)}, u32[]{:S(2)}, u32[]{:S(2)}) collective-permute-start(bf16[2,256,640]{2,1,0:T(8,128)(2,1)S(1)} %pad_maximum_fusion.21), channel_id=1, source_target_pairs={{0,4},{4,0},{8,12},{12,8},{16,24},{20,28},{24,16},{28,20},{1,5},{5... | collective-permute-start | bytes 1966088 | tf_op jit(solution)/shard_map/ppermute | solution.py:115
  457.1 8.0 %collective-permute-start.45 = (bf16[4,128,640]{2,1,0:T(8,128)(2,1)S(1)}, bf16[4,128,640]{2,1,0:T(8,128)(2,1)S(1)}, u32[]{:S(2)}, u32[]{:S(2)}) collective-permute-start(bf16[4,128,640]{2,1,0:T(8,128)(2,1)S(1)} %dynamic-slice_bitcast_fusion.6), channel_id=1, source_target_pairs={{0,16},{16,0},{1,17},{17,1},{2,18},{18,2},{3,19},{19,3},{4,20},{20... | collective-permute-start | bytes 1966088 | tf_op jit(solution)/shard_map/ppermute | solution.py:119
  457.2 7.1 %collective-permute-start.41 = (bf16[256,640]{1,0:T(8,128)(2,1)S(1)}, bf16[256,640]{1,0:T(8,128)(2,1)S(1)}, u32[]{:S(2)}, u32[]{:S(2)}) collective-permute-start(bf16[256,640]{1,0:T(8,128)(2,1)S(1)} %get-tuple-element.92), channel_id=1, source_target_pairs={{0,8},{4,12},{8,0},{12,4},{16,20},{20,16},{24,28},{28,24},{1,9},{5... | collective-permute-start | bytes 983048 | tf_op jit(solution)/shard_map/ppermute | solution.py:115
  459.0 15.1 %collective-permute-start.42 = (bf16[4,96,1536]{2,1,0:T(8,128)(2,1)}, bf16[4,96,1536]{2,1,0:T(8,128)(2,1)}, u32[]{:S(2)}, u32[]{:S(2)}) collective-permute-start(bf16[4,96,1536]{2,1,0:T(8,128)(2,1)} %dynamic-slice_bitcast_fusion.4), channel_id=1, source_target_pairs={{0,16},{16,0},{1,17},{17,1},{2,18},{18,2},{3,19},{19,3},{4,20},{20... | collective-permute-start | bytes 3538952 | tf_op jit(solution)/shard_map/ppermute | solution.py:119
  460.6 12.3 %collective-permute-start.40 = (bf16[80,4096]{1,0:T(8,128)(2,1)S(1)}, bf16[80,4096]{1,0:T(8,128)(2,1)S(1)}, u32[]{:S(2)}, u32[]{:S(2)}) collective-permute-start(bf16[80,4096]{1,0:T(8,128)(2,1)S(1)} %get-tuple-element.90), channel_id=1, source_target_pairs={{0,8},{4,12},{8,0},{12,4},{16,20},{20,16},{24,28},{28,24},{1,9},{5... | collective-permute-start | bytes 1966088 | tf_op jit(solution)/shard_map/ppermute | solution.py:115
  461.5 17.1 %collective-permute-start.39 = (bf16[512,640]{1,0:T(8,128)(2,1)}, bf16[512,640]{1,0:T(8,128)(2,1)S(1)}, u32[]{:S(2)}, u32[]{:S(2)}) collective-permute-start(bf16[512,640]{1,0:T(8,128)(2,1)} %select_convert_fusion), channel_id=1, source_target_pairs={{0,16},{16,0},{1,17},{17,1},{2,18},{18,2},{3,19},{19,3},{4,20},{20... | collective-permute-start | bytes 1966088 | tf_op jit(solution)/shard_map/ppermute | solution.py:119
  467.2 11.7 %collective-permute-start.46 = (bf16[2,128,640]{2,1,0:T(8,128)(2,1)}, bf16[2,128,640]{2,1,0:T(8,128)(2,1)}, u32[]{:S(2)}, u32[]{:S(2)}) collective-permute-start(bf16[2,128,640]{2,1,0:T(8,128)(2,1)} %pad_maximum_fusion.33), channel_id=1, source_target_pairs={{0,4},{4,0},{8,12},{12,8},{16,24},{20,28},{24,16},{28,20},{1,5},{5... | collective-permute-start | bytes 983048 | tf_op jit(solution)/shard_map/ppermute | solution.py:115
  473.9 107.3 %all-reduce.19.cloned.1.call-start = ((), (), s32[]{:S(2)}) async-start(), calls=%async_computation | async-start | bytes 917504 | tf_op jit(solution)/shard_map/psum | solution.py:543
  476.3 10.8 %collective-permute-start.43 = (bf16[2,96,1536]{2,1,0:T(8,128)(2,1)S(1)}, bf16[2,96,1536]{2,1,0:T(8,128)(2,1)S(1)}, u32[]{:S(2)}, u32[]{:S(2)}) collective-permute-start(bf16[2,96,1536]{2,1,0:T(8,128)(2,1)S(1)} %pad_maximum_fusion.27), channel_id=1, source_target_pairs={{0,4},{4,0},{8,12},{12,8},{16,24},{20,28},{24,16},{28,20},{1,5},{5... | collective-permute-start | bytes 1769480 | tf_op jit(solution)/shard_map/ppermute | solution.py:115
  479.9 10.9 %collective-permute-start.47 = (bf16[128,640]{1,0:T(8,128)(2,1)S(1)}, bf16[128,640]{1,0:T(8,128)(2,1)S(1)}, u32[]{:S(2)}, u32[]{:S(2)}) collective-permute-start(bf16[128,640]{1,0:T(8,128)(2,1)S(1)} %fusion.183), channel_id=1, source_target_pairs={{0,8},{4,12},{8,0},{12,4},{16,20},{20,16},{24,28},{28,24},{1,9},{5... | collective-permute-start | bytes 491528 | tf_op jit(solution)/shard_map/ppermute | solution.py:115
  487.3 6.8 %collective-permute-start.44 = (bf16[96,1536]{1,0:T(8,128)(2,1)S(1)}, bf16[96,1536]{1,0:T(8,128)(2,1)S(1)}, u32[]{:S(2)}, u32[]{:S(2)}) collective-permute-start(bf16[96,1536]{1,0:T(8,128)(2,1)S(1)} %fusion.148), channel_id=1, source_target_pairs={{0,8},{4,12},{8,0},{12,4},{16,20},{20,16},{24,28},{28,24},{1,9},{5... | collective-permute-start | bytes 884744 | tf_op jit(solution)/shard_map/ppermute | solution.py:115
  490.9 50.2 %copy-start.88 = (bf16[256,640]{1,0:T(8,128)(2,1)S(1)}, bf16[256,640]{1,0:T(8,128)(2,1)}, u32[]{:S(2)}) copy-start(bf16[256,640]{1,0:T(8,128)(2,1)} %get-tuple-element.106) | copy-start | bytes 983044
  490.9 50.4 %copy-start.75 = (bf16[80,4096]{1,0:T(8,128)(2,1)S(1)}, bf16[80,4096]{1,0:T(8,128)(2,1)}, u32[]{:S(2)}) copy-start(bf16[80,4096]{1,0:T(8,128)(2,1)} %get-tuple-element.104) | copy-start | bytes 1966084
  541.1 1.9 collective-permute-start.51
  541.3 44.9 %collective-permute-start.50 = (bf16[80,4096]{1,0:T(8,128)(2,1)S(1)}, bf16[80,4096]{1,0:T(8,128)(2,1)S(1)}, u32[]{:S(2)}, u32[]{:S(2)}) collective-permute-start(bf16[80,4096]{1,0:T(8,128)(2,1)S(1)} %broadcast_select_fusion), channel_id=1, source_target_pairs={{0,16},{16,0},{1,17},{17,1},{2,18},{18,2},{3,19},{19,3},{4,20},{20... | collective-permute-start | bytes 1966088 | tf_op jit(solution)/shard_map/ppermute | solution.py:119
  581.2 3.1 collective-permute-start.49
  582.4 5.9 collective-permute-start.48
  (205 other events, 1103.7 us)
Sparse Core Ops, SparseCore 0:
  400.1 52.3 all-reduce.22
  474.0 67.0 all-reduce.20
  544.2 36.9 all-reduce.18
where the time goes:
time: 607 us; the launch traced here: 598 us
  waiting for transfers between devices  218 us (36%)
  other arithmetic  111 us (18%)
  matrix products  102 us (17%)
  local copies, waits for them, and re-layouts  94.2 us (16%)
  starting transfers between devices  54.6 us (9%)
  between operations  17.5 us (3%)
    ppermute x28, waiting for transfers between devices, hop(): return lax.ppermute(block, ('section', 'fsdp'), route)  104 us
    psum x1, waiting for transfers between devices, local(): rest = [lax.psum(total, 'rep') for total in rest]  46.2 us
    unnamed x432, local copies, waits for them, and re-layouts  36.1 us
    psum x1, waiting for transfers between devices, local(): lower_attn = [lax.psum(total, 'rep') for total in lower_attn]  36 us
    ppermute x28, starting transfers between devices, hop(): return lax.ppermute(block, ('section', 'fsdp'), route)  35.2 us
    dot_general x8, matrix products, dot_transposed(): lax.dot_general(left, right, (((1,), (1,)), ((), ())), preferred_element_...  31.9 us
    ppermute x4, waiting for transfers between devices, from_behind(): return lax.ppermute(block, axis, route)  30.6 us
    dot_general x8, matrix products, outer_dot(): lax.dot_general(left, right, (((0,), (0,)), ((), ())), preferred_element_...  25.9 us
  transfers between devices with their start and end apart: 55, of which 19 were waited for; matrix products, arithmetic and copies ran while one was open for 32% of the time, Pallas kernels for 0%

commit v1 on v0

--- a/solution.py
+++ b/solution.py
@@ -522,8 +522,8 @@
     d_residual, upper_ff, upper_attn = lax.optimization_barrier(
         (d_residual, upper_ff, upper_attn)
     )
-    upper_ff = [lax.psum(total, "rep") for total in upper_ff]
     upper_attn = [add_far(pair) for pair in upper_attn]
+    upper_sums = [lax.psum(total, "rep") for total in upper_attn + upper_ff]
     lower_ff = [add_near(add_cores(row_blocks(grad))) for grad in lower_ff]
     d_tokens, lower_attn, lower_attn_gains = attn_backward(
         d_residual, lower_state, lower_params, layout
@@ -532,17 +532,10 @@
         with_gains(row_blocks(lower_attn[0]), lower_attn_gains, lower_ff_gains),
         row_blocks(lower_attn[1]),
     ]
-    d_tokens, lower_attn, lower_ff, upper_attn = lax.optimization_barrier(
-        (d_tokens, lower_attn, lower_ff, upper_attn)
-    )
     lower_ff = [add_far(pair) for pair in lower_ff]
-    upper_ff, rest = lax.optimization_barrier((upper_ff, upper_attn + lower_ff))
-    rest = [lax.psum(total, "rep") for total in rest]
     lower_attn = [add_far(add_near(add_cores(blocks))) for blocks in lower_attn]
-    rest, lower_attn = lax.optimization_barrier((rest, lower_attn))
-    lower_attn = [lax.psum(total, "rep") for total in lower_attn]
-    upper_sums = rest[:2] + upper_ff
-    lower_sums = lower_attn + rest[2:]
+    upper_sums, lower_sums = lax.optimization_barrier((upper_sums, lower_attn + lower_ff))
+    lower_sums = [lax.psum(total, "rep") for total in lower_sums]
 
     def for_layers(lower_value, upper_value):
         mine = jnp.where(first_core, lower_value, upper_value)

time: 607 us -> 594 us (0.979)
  waiting for transfers between devices: 218 us -> 203 us
    psum x3 -> x2, waiting for transfers between devices: 82.2 us -> 59.9 us  [the longest x1 59.9 us: local(): lower_sums = [lax.psum(total, 'rep') for total in lower_sums]]
    unnamed x432 -> x428, local copies, waits for them, and re-layouts: 36.1 us -> 33.9 us
  transfers between devices with their start and end apart: 55 -> 54, of which waited for: 19 -> 22; matrix products, arithmetic and copies ran while one was open for 32% -> 37% of each run, Pallas kernels for 0% -> 0%
where the time goes in v1:
time: 594 us; the launch traced here: 585 us
  waiting for transfers between devices  203 us (34%)
  other arithmetic  117 us (20%)
  matrix products  105 us (18%)
  local copies, waits for them, and re-layouts  92.1 us (16%)
  starting transfers between devices  50.9 us (9%)
  between operations  17.6 us (3%)
    ppermute x28, waiting for transfers between devices, hop(): return lax.ppermute(block, ('section', 'fsdp'), route)  109 us
    psum x1, waiting for transfers between devices, local(): lower_sums = [lax.psum(total, 'rep') for total in lower_sums]  59.9 us
    dot_general x8, matrix products, dot_transposed(): lax.dot_general(left, right, (((1,), (1,)), ((), ())), preferred_element_...  34.9 us
    ppermute x4, waiting for transfers between devices, from_behind(): return lax.ppermute(block, axis, route)  34.5 us
    ppermute x28, starting transfers between devices, hop(): return lax.ppermute(block, ('section', 'fsdp'), route)  33.9 us
    unnamed x428, local copies, waits for them, and re-layouts  33.9 us
    dot_general x8, matrix products, outer_dot(): lax.dot_general(left, right, (((0,), (0,)), ((), ())), preferred_element_...  23.4 us
    dynamic_update_slice x16, local copies, waits for them, and re-layouts, gather_rows(): held = lax.dynamic_update_index_in_dim(held, piece, place, 0)  16.5 us
  transfers between devices with their start and end apart: 54, of which 22 were waited for; matrix products, arithmetic and copies ran while one was open for 37% of the time, Pallas kernels for 0%

profile of v1, /device:TPU:0, one launch (start us, length us, event | category | flops | bytes accessed | tf_op | source)
XLA Modules:
  0.0 585.1 jit_solution(243120747688649993)
XLA Ops:
  16.5 2.6 collective-permute-start.1
  23.1 26.6 %collective-permute-done.4 = bf16[400,640]{1,0:T(8,128)(2,1)} collective-permute-done((bf16[400,640]{1,0:T(8,128)(2,1)S(1)}, bf16[400,640]{1,0:T(8,128)(2,1)}, u32[]{:S(2)}, u32[]{:S(2)}) %collective-permute-start.4) | collective-permute-done | bytes 512032 | tf_op jit(solution)/shard_map/ppermute | solution.py:115
  53.7 2.1 broadcast.590.clone
  56.8 2.1 bitcast_dynamic-update-slice_fusion.6
  59.0 2.3 bitcast_dynamic-update-slice_fusion.5
  61.2 8.5 %collective-permute-done.7 = bf16[80,5632]{1,0:T(8,128)(2,1)S(1)} collective-permute-done((bf16[80,5632]{1,0:T(8,128)(2,1)}, bf16[80,5632]{1,0:T(8,128)(2,1)S(1)}, u32[]{:S(2)}, u32[]{:S(2)}) %collective-permute-start.7) | collective-permute-done | bytes 901152 | tf_op jit(solution)/shard_map/ppermute | solution.py:115
  94.0 2.4 copy.149
  96.4 2.7 multiply_reduce_fusion.5
  101.1 4.1 collective-permute-start.9
  105.2 2.9 select_bitcast_fusion.3
  110.9 8.7 %collective-permute-done.9 = bf16[512,512]{0,1:T(8,128)(2,1)S(1)} collective-permute-done((bf16[512,512]{0,1:T(8,128)(2,1)S(1)}, bf16[512,512]{0,1:T(8,128)(2,1)S(1)}, u32[]{:S(2)}, u32[]{:S(2)}) %collective-permute-start.9) | collective-permute-done | bytes 524320 | tf_op jit(solution)/shard_map/ppermute | solution.py:20
  122.3 2.0 multiply_convert_fusion.8
  130.2 2.3 collective-permute-start.15
  134.5 2.1 broadcast.590
  137.5 2.2 bitcast_dynamic-update-slice_fusion.2
  141.0 2.2 bitcast_dynamic-update-slice_fusion.1
  145.2 4.2 collective-permute-done.16
  151.0 4.3 multiply_convert_fusion.7
  155.4 2.4 copy.194
  157.8 4.2 multiply_reduce_fusion.17
  176.5 3.1 select_bitcast_fusion.1
  182.8 4.2 collective-permute-start.18
  189.9 8.5 %collective-permute-done.18 = bf16[512,512]{0,1:T(8,128)(2,1)S(1)} collective-permute-done((bf16[512,512]{0,1:T(8,128)(2,1)S(1)}, bf16[512,512]{0,1:T(8,128)(2,1)S(1)}, u32[]{:S(2)}, u32[]{:S(2)}) %collective-permute-start.18) | collective-permute-done | bytes 524320 | tf_op jit(solution)/shard_map/ppermute | solution.py:20
  199.2 2.1 fusion.21
  201.3 2.0 multiply_convert_fusion.5
  210.8 3.9 multiply_convert_fusion.4
  217.7 3.6 convolution_convert_fusion.3
  221.4 8.0 %fusion.9 = (bf16[512,2048]{1,0:T(8,128)(2,1)S(1)}, bf16[512,2048]{1,0:T(8,128)(2,1)S(1)}) fusion(f32[512,2048]{1,0:T(8,128)S(1)} %fusion.26, f32[512,2048]{1,0:T(8,128)} %get-tuple-element.293, bf16[2048,640]{1,0:T(8,128)(2,1)S(1)} %bitcast.546, f32[512,640]{1,0:T(8,128)S(1)} %get-tuple-element.295, f32[512]{0:T(512)S(1)} %multiply_multiply_fusion.19, ...), kind=kOutput, calls=%fused_computation.27 | convolution fusion | flops 1375928320 | bytes 17178628 | tf_op jit(solution)/shard_map/dot_general | solution.py:84
  229.4 4.9 convolution_convert_fusion.1
  234.3 5.2 multiply_reduce_fusion.9
  239.5 2.3 copy.173
  242.4 3.8 multiply_reduce_fusion.10
  250.0 2.0 convolution_convert_fusion.9
  257.6 2.4 copy.255
  260.1 2.0 convert_multiply_fusion.9
  276.8 2.1 multiply_reduce_fusion.2
  279.5 2.3 fusion.32
  281.8 9.3 %collective-permute-done.21 = bf16[512,512]{0,1:T(8,128)(2,1)} collective-permute-done((bf16[512,512]{0,1:T(8,128)(2,1)}, bf16[512,512]{0,1:T(8,128)(2,1)}, u32[]{:S(2)}, u32[]{:S(2)}) %collective-permute-start.21) | collective-permute-done | bytes 524320 | tf_op jit(solution)/shard_map/ppermute | solution.py:20
  298.5 2.7 convolution_convert_fusion.5
  304.8 2.7 collective-permute-start.31
  311.9 2.7 convert_add_fusion.1
  317.8 2.2 collective-permute-done.25
  321.2 5.1 collective-permute-done.29
  327.5 12.8 %collective-permute-done.23 = bf16[2,80,4096]{2,1,0:T(8,128)(2,1)S(1)} collective-permute-done((bf16[2,80,4096]{2,1,0:T(8,128)(2,1)S(1)}, bf16[2,80,4096]{2,1,0:T(8,128)(2,1)S(1)}, u32[]{:S(2)}, u32[]{:S(2)}) %collective-permute-start.23) | collective-permute-done | bytes 1310752 | tf_op jit(solution)/shard_map/ppermute | solution.py:115
  344.1 2.1 convolution_convert_fusion.2
  347.0 8.9 %fusion.5 = (bf16[512,2048]{1,0:T(8,128)(2,1)S(1)}, bf16[512,2048]{1,0:T(8,128)(2,1)S(1)}) fusion(f32[512,2048]{1,0:T(8,128)S(1)} %copy-done.202, f32[512,2048]{1,0:T(8,128)} %get-tuple-element.281, bf16[2048,640]{1,0:T(8,128)(2,1)S(1)} %bitcast.544, bf16[512,640]{1,0:T(8,128)(2,1)S(1)} %get-tuple-element.174, f32[512,640]{1,0:T(8,128)S(1)} %copy-done.56, ...), kind=kOutput, calls=%fused_computation.23 | convolution fusion | flops 1375928320 | bytes 17177088 | tf_op jit(solution)/shard_map/dot_general | solution.py:84
  356.0 3.3 convolution_convert_fusion
  359.4 4.5 multiply_reduce_fusion.6
  371.6 3.1 collective-permute-done.27
  376.6 5.2 collective-permute-done.26
  381.8 2.1 add_convert_fusion.2
  385.6 2.0 convolution_convert_fusion.8
  389.6 2.7 copy.258
  419.1 8.0 %collective-permute-done.32 = bf16[512,512]{0,1:T(8,128)(2,1)} collective-permute-done((bf16[512,512]{0,1:T(8,128)(2,1)}, bf16[512,512]{0,1:T(8,128)(2,1)}, u32[]{:S(2)}, u32[]{:S(2)}) %collective-permute-start.32) | collective-permute-done | bytes 524320 | tf_op jit(solution)/shard_map/ppermute | solution.py:20
  428.3 2.7 slice_add_fusion.13
  433.6 2.8 convolution_convert_fusion.4
  436.4 2.6 fusion.52
  442.6 2.7 collective-permute-start.40
  447.5 2.8 collective-permute-done.40
  451.9 2.7 convert_add_fusion
  460.3 23.2 %collective-permute-done.37 = bf16[2,96,1536]{2,1,0:T(8,128)(2,1)S(1)} collective-permute-done((bf16[2,96,1536]{2,1,0:T(8,128)(2,1)S(1)}, bf16[2,96,1536]{2,1,0:T(8,128)(2,1)S(1)}, u32[]{:S(2)}, u32[]{:S(2)}) %collective-permute-start.37) | collective-permute-done | bytes 589856 | tf_op jit(solution)/shard_map/ppermute | solution.py:115
  487.1 3.4 collective-permute-done.38
  491.3 6.2 %collective-permute-done.44 = bf16[80,4096]{1,0:T(8,128)(2,1)S(1)} collective-permute-done((bf16[80,4096]{1,0:T(8,128)(2,1)S(1)}, bf16[80,4096]{1,0:T(8,128)(2,1)S(1)}, u32[]{:S(2)}, u32[]{:S(2)}) %collective-permute-start.44) | collective-permute-done | bytes 655392 | tf_op jit(solution)/shard_map/ppermute | solution.py:115
  505.0 59.9 %all-reduce.17.cloned.1.call-done = (bf16[96,1536]{1,0:T(8,128)(2,1)}, bf16[128,640]{1,0:T(8,128)(2,1)}, bf16[80,4096]{1,0:T(8,128)(2,1)}, bf16[256,640]{1,0:T(8,128)(2,1)}) async-done(((bf16[96,1536]{1,0:T(8,128)(2,1)}, bf16[128,640]{1,0:T(8,128)(2,1)}, bf16[80,4096]{1,0:T(8,128)(2,1)}, bf16[256,640]{1,0:T(8,128)(2,1)}), (bf16[96,1536]{1,0:T(8,128)(2,1)}, bf16[128,640]{1,0:T(8,128)(2,1)}, ...) | async-done | bytes 1441808 | tf_op jit(solution)/shard_map/psum | solution.py:538
  (820 shorter events, 225.9 us)
Async XLA Ops:
  7.2 491.3 %all-reduce.19.cloned.1.call-start = ((), (), s32[]{:S(2)}) async-start(), calls=%async_computation.1 | async-start | bytes 2883584 | tf_op jit(solution)/shard_map/psum | solution.py:526
  11.5 3.5 collective-permute-start
  14.5 6.1 %collective-permute-start.3 = (bf16[400,640]{1,0:T(8,128)(2,1)}, bf16[400,640]{1,0:T(8,128)(2,1)}, u32[]{:S(2)}, u32[]{:S(2)}) collective-permute-start(bf16[400,640]{1,0:T(8,128)(2,1)} %dynamic-slice_bitcast_fusion.7), channel_id=1, source_target_pairs={{0,16},{16,0},{1,17},{17,1},{2,18},{18,2},{3,19},{19,3},{4,20},{20... | collective-permute-start | bytes 1536008 | tf_op jit(solution)/shard_map/ppermute | solution.py:119
  16.5 61.0 %copy-start.65 = (bf16[80,5632]{1,0:T(8,128)(2,1)}, bf16[80,5632]{1,0:T(8,128)(2,1)S(1)}, u32[]{:S(2)}) copy-start(bf16[80,5632]{1,0:T(8,128)(2,1)S(1)} %get-tuple-element.58) | copy-start | bytes 2703364
  16.5 34.2 %collective-permute-start.1 = (bf16[80,5632]{1,0:T(8,128)(2,1)S(1)}, bf16[80,5632]{1,0:T(8,128)(2,1)}, u32[]{:S(2)}, u32[]{:S(2)}) collective-permute-start(bf16[80,5632]{1,0:T(8,128)(2,1)S(1)} %get-tuple-element.49), channel_id=1, source_target_pairs={{0,4},{4,0},{8,12},{12,8},{16,24},{20,28},{24,16},{28,20},{1,5},{5... | collective-permute-start | bytes 2703368 | tf_op jit(solution)/shard_map/ppermute | solution.py:115
  19.1 31.7 %collective-permute-start.2 = (bf16[80,5632]{1,0:T(8,128)(2,1)S(1)}, bf16[80,5632]{1,0:T(8,128)(2,1)}, u32[]{:S(2)}, u32[]{:S(2)}) collective-permute-start(bf16[80,5632]{1,0:T(8,128)(2,1)S(1)} %get-tuple-element.49), channel_id=1, source_target_pairs={{0,8},{4,12},{8,0},{12,4},{16,20},{20,16},{24,28},{28,24},{1,9},{5... | collective-permute-start | bytes 2703368 | tf_op jit(solution)/shard_map/ppermute | solution.py:115
  22.5 27.2 %collective-permute-start.4 = (bf16[400,640]{1,0:T(8,128)(2,1)S(1)}, bf16[400,640]{1,0:T(8,128)(2,1)}, u32[]{:S(2)}, u32[]{:S(2)}) collective-permute-start(bf16[400,640]{1,0:T(8,128)(2,1)S(1)} %get-tuple-element.46), channel_id=1, source_target_pairs={{0,4},{4,0},{8,12},{12,8},{16,24},{20,28},{24,16},{28,20},{1,5},{5... | collective-permute-start | bytes 1536008 | tf_op jit(solution)/shard_map/ppermute | solution.py:115
  23.1 27.7 %collective-permute-start.5 = (bf16[400,640]{1,0:T(8,128)(2,1)S(1)}, bf16[400,640]{1,0:T(8,128)(2,1)S(1)}, u32[]{:S(2)}, u32[]{:S(2)}) collective-permute-start(bf16[400,640]{1,0:T(8,128)(2,1)S(1)} %get-tuple-element.46), channel_id=1, source_target_pairs={{0,8},{4,12},{8,0},{12,4},{16,20},{20,16},{24,28},{28,24},{1,9},{5... | collective-permute-start | bytes 1536008 | tf_op jit(solution)/shard_map/ppermute | solution.py:115
  50.8 21.2 %collective-permute-start.6 = (bf16[400,640]{1,0:T(8,128)(2,1)}, bf16[400,640]{1,0:T(8,128)(2,1)S(1)}, u32[]{:S(2)}, u32[]{:S(2)}) collective-permute-start(bf16[400,640]{1,0:T(8,128)(2,1)} %collective-permute-done.4), channel_id=1, source_target_pairs={{0,8},{4,12},{8,0},{12,4},{16,20},{20,16},{24,28},{28,24},{1,9},{5... | collective-permute-start | bytes 1536008 | tf_op jit(solution)/shard_map/ppermute | solution.py:115
  52.8 17.0 %collective-permute-start.7 = (bf16[80,5632]{1,0:T(8,128)(2,1)}, bf16[80,5632]{1,0:T(8,128)(2,1)S(1)}, u32[]{:S(2)}, u32[]{:S(2)}) collective-permute-start(bf16[80,5632]{1,0:T(8,128)(2,1)} %collective-permute-done.1), channel_id=1, source_target_pairs={{0,8},{4,12},{8,0},{12,4},{16,20},{20,16},{24,28},{28,24},{1,9},{5... | collective-permute-start | bytes 2703368 | tf_op jit(solution)/shard_map/ppermute | solution.py:115
  70.8 17.2 %collective-permute-start.8 = (bf16[4,80,5632]{2,1,0:T(8,128)(2,1)}, bf16[4,80,5632]{2,1,0:T(8,128)(2,1)}, u32[]{:S(2)}, u32[]{:S(2)}) collective-permute-start(bf16[4,80,5632]{2,1,0:T(8,128)(2,1)} %bitcast_dynamic-update-slice_fusion.4), channel_id=1, source_target_pairs={{0,16},{16,0},{1,17},{17,1},{2,18},{18,2},{3,19},{19,3},{4,20},{20... | collective-permute-start | bytes 10813448 | tf_op jit(solution)/shard_map/ppermute | solution.py:119
  72.1 8.5 %collective-permute-start.10 = (bf16[4,400,640]{2,1,0:T(8,128)(2,1)S(1)}, bf16[4,400,640]{2,1,0:T(8,128)(2,1)}, u32[]{:S(2)}, u32[]{:S(2)}) collective-permute-start(bf16[4,400,640]{2,1,0:T(8,128)(2,1)S(1)} %bitcast_dynamic-update-slice_fusion.12), channel_id=1, source_target_pairs={{0,16},{16,0},{1,17},{17,1},{2,18},{18,2},{3,19},{19,3},{4,20},{20... | collective-permute-start | bytes 6144008 | tf_op jit(solution)/shard_map/ppermute | solution.py:119
  75.8 46.6 %copy-start.47 = (pred[512,512]{0,1:T(8,128)(4,1)}, pred[512,512]{0,1:T(8,128)(4,1)S(1)}, u32[]{:S(2)}) copy-start(pred[512,512]{0,1:T(8,128)(4,1)S(1)} %get-tuple-element.266) | copy-start | bytes 786436
  75.8 46.6 %copy-start.49 = (pred[512,512]{0,1:T(8,128)(4,1)}, pred[512,512]{0,1:T(8,128)(4,1)S(1)}, u32[]{:S(2)}) copy-start(pred[512,512]{0,1:T(8,128)(4,1)S(1)} %get-tuple-element.267) | copy-start | bytes 786436
  75.8 54.4 %collective-permute-start.11 = (bf16[80,5632]{1,0:T(8,128)(2,1)S(1)}, bf16[80,5632]{1,0:T(8,128)(2,1)}, u32[]{:S(2)}, u32[]{:S(2)}) collective-permute-start(bf16[80,5632]{1,0:T(8,128)(2,1)S(1)} %get-tuple-element.58), channel_id=1, source_target_pairs={{0,4},{4,0},{8,12},{12,8},{16,24},{20,28},{24,16},{28,20},{1,5},{5... | collective-permute-start | bytes 2703368 | tf_op jit(solution)/shard_map/ppermute | solution.py:115
  77.5 52.6 %collective-permute-start.12 = (bf16[80,5632]{1,0:T(8,128)(2,1)S(1)}, bf16[80,5632]{1,0:T(8,128)(2,1)}, u32[]{:S(2)}, u32[]{:S(2)}) collective-permute-start(bf16[80,5632]{1,0:T(8,128)(2,1)S(1)} %get-tuple-element.58), channel_id=1, source_target_pairs={{0,8},{4,12},{8,0},{12,4},{16,20},{20,16},{24,28},{28,24},{1,9},{5... | collective-permute-start | bytes 2703368 | tf_op jit(solution)/shard_map/ppermute | solution.py:115
  79.4 50.8 %collective-permute-start.13 = (bf16[400,640]{1,0:T(8,128)(2,1)}, bf16[400,640]{1,0:T(8,128)(2,1)}, u32[]{:S(2)}, u32[]{:S(2)}) collective-permute-start(bf16[400,640]{1,0:T(8,128)(2,1)} %get-tuple-element.55), channel_id=1, source_target_pairs={{0,4},{4,0},{8,12},{12,8},{16,24},{20,28},{24,16},{28,20},{1,5},{5... | collective-permute-start | bytes 1536008 | tf_op jit(solution)/shard_map/ppermute | solution.py:115
  80.4 48.5 %copy-start.131 = (f32[640]{0:T(1024)}, f32[640]{0:T(1024)S(1)}, u32[]{:S(2)}) copy-start(f32[640]{0:T(1024)S(1)} %mul.1173) | copy-start | bytes 7684
  80.5 62.7 %copy-start.133 = (f32[640]{0:T(1024)}, f32[640]{0:T(1024)S(1)}, u32[]{:S(2)}) copy-start(f32[640]{0:T(1024)S(1)} %mul.1179) | copy-start | bytes 7684
  80.6 82.1 %copy-start.135 = (f32[640]{0:T(1024)}, f32[640]{0:T(1024)S(1)}, u32[]{:S(2)}) copy-start(f32[640]{0:T(1024)S(1)} %mul.1192) | copy-start | bytes 7684
  80.6 49.6 %collective-permute-start.14 = (bf16[400,640]{1,0:T(8,128)(2,1)}, bf16[400,640]{1,0:T(8,128)(2,1)}, u32[]{:S(2)}, u32[]{:S(2)}) collective-permute-start(bf16[400,640]{1,0:T(8,128)(2,1)} %get-tuple-element.55), channel_id=1, source_target_pairs={{0,8},{4,12},{8,0},{12,4},{16,20},{20,16},{24,28},{28,24},{1,9},{5... | collective-permute-start | bytes 1536008 | tf_op jit(solution)/shard_map/ppermute | solution.py:115
  101.1 18.4 %collective-permute-start.9 = (bf16[512,512]{0,1:T(8,128)(2,1)S(1)}, bf16[512,512]{0,1:T(8,128)(2,1)S(1)}, u32[]{:S(2)}, u32[]{:S(2)}) collective-permute-start(bf16[512,512]{0,1:T(8,128)(2,1)S(1)} %pad_maximum_fusion.27), channel_id=1, source_target_pairs={{0,4},{4,8},{8,12},{1,5},{5,9},{9,13},{2,6},{6,10},{10,14},{3,7},{... | collective-permute-start | bytes 1572872 | tf_op jit(solution)/shard_map/ppermute | solution.py:20
  130.2 20.2 %collective-permute-start.15 = (bf16[400,640]{1,0:T(8,128)(2,1)}, bf16[400,640]{1,0:T(8,128)(2,1)S(1)}, u32[]{:S(2)}, u32[]{:S(2)}) collective-permute-start(bf16[400,640]{1,0:T(8,128)(2,1)} %collective-permute-done.13), channel_id=1, source_target_pairs={{0,8},{4,12},{8,0},{12,4},{16,20},{20,16},{24,28},{28,24},{1,9},{5... | collective-permute-start | bytes 1536008 | tf_op jit(solution)/shard_map/ppermute | solution.py:115
  133.9 15.4 %collective-permute-start.16 = (bf16[80,5632]{1,0:T(8,128)(2,1)}, bf16[80,5632]{1,0:T(8,128)(2,1)S(1)}, u32[]{:S(2)}, u32[]{:S(2)}) collective-permute-start(bf16[80,5632]{1,0:T(8,128)(2,1)} %collective-permute-done.11), channel_id=1, source_target_pairs={{0,8},{4,12},{8,0},{12,4},{16,20},{20,16},{24,28},{28,24},{1,9},{5... | collective-permute-start | bytes 2703368 | tf_op jit(solution)/shard_map/ppermute | solution.py:115
  150.4 21.2 %collective-permute-start.17 = (bf16[4,80,5632]{2,1,0:T(8,128)(2,1)}, bf16[4,80,5632]{2,1,0:T(8,128)(2,1)}, u32[]{:S(2)}, u32[]{:S(2)}) collective-permute-start(bf16[4,80,5632]{2,1,0:T(8,128)(2,1)} %bitcast_dynamic-update-slice_fusion), channel_id=1, source_target_pairs={{0,16},{16,0},{1,17},{17,1},{2,18},{18,2},{3,19},{19,3},{4,20},{20... | collective-permute-start | bytes 10813448 | tf_op jit(solution)/shard_map/ppermute | solution.py:119
  150.5 16.4 %collective-permute-start.19 = (bf16[4,400,640]{2,1,0:T(8,128)(2,1)S(1)}, bf16[4,400,640]{2,1,0:T(8,128)(2,1)}, u32[]{:S(2)}, u32[]{:S(2)}) collective-permute-start(bf16[4,400,640]{2,1,0:T(8,128)(2,1)S(1)} %bitcast_dynamic-update-slice_fusion.8), channel_id=1, source_target_pairs={{0,16},{16,0},{1,17},{17,1},{2,18},{18,2},{3,19},{19,3},{4,20},{20... | collective-permute-start | bytes 6144008 | tf_op jit(solution)/shard_map/ppermute | solution.py:119
  182.8 15.6 %collective-permute-start.18 = (bf16[512,512]{0,1:T(8,128)(2,1)S(1)}, bf16[512,512]{0,1:T(8,128)(2,1)S(1)}, u32[]{:S(2)}, u32[]{:S(2)}) collective-permute-start(bf16[512,512]{0,1:T(8,128)(2,1)S(1)} %pad_maximum_fusion.28), channel_id=1, source_target_pairs={{0,4},{4,8},{8,12},{1,5},{5,9},{9,13},{2,6},{6,10},{10,14},{3,7},{... | collective-permute-start | bytes 1572872 | tf_op jit(solution)/shard_map/ppermute | solution.py:20
  255.5 52.0 %collective-permute-start.24 = (bf16[4,256,640]{2,1,0:T(8,128)(2,1)}, bf16[4,256,640]{2,1,0:T(8,128)(2,1)}, u32[]{:S(2)}, u32[]{:S(2)}) collective-permute-start(bf16[4,256,640]{2,1,0:T(8,128)(2,1)} %dynamic-slice_bitcast_fusion.3), channel_id=1, source_target_pairs={{0,16},{16,0},{1,17},{17,1},{2,18},{18,2},{3,19},{19,3},{4,20},{20... | collective-permute-start | bytes 3932168 | tf_op jit(solution)/shard_map/ppermute | solution.py:119
  257.1 54.8 %collective-permute-start.22 = (bf16[4,80,4096]{2,1,0:T(8,128)(2,1)}, bf16[4,80,4096]{2,1,0:T(8,128)(2,1)}, u32[]{:S(2)}, u32[]{:S(2)}) collective-permute-start(bf16[4,80,4096]{2,1,0:T(8,128)(2,1)} %dynamic-slice_bitcast_fusion.1), channel_id=1, source_target_pairs={{0,16},{16,0},{1,17},{17,1},{2,18},{18,2},{3,19},{19,3},{4,20},{20... | collective-permute-start | bytes 7864328 | tf_op jit(solution)/shard_map/ppermute | solution.py:119
  274.3 16.8 %collective-permute-start.21 = (bf16[512,512]{0,1:T(8,128)(2,1)}, bf16[512,512]{0,1:T(8,128)(2,1)}, u32[]{:S(2)}, u32[]{:S(2)}) collective-permute-start(bf16[512,512]{0,1:T(8,128)(2,1)} %pad_maximum_fusion.29), channel_id=1, source_target_pairs={{4,0},{8,4},{12,8},{5,1},{9,5},{13,9},{6,2},{10,6},{14,10},{7,3},{... | collective-permute-start | bytes 1572872 | tf_op jit(solution)/shard_map/ppermute | solution.py:20
  276.5 26.7 %collective-permute-start.30 = (bf16[4,128,640]{2,1,0:T(8,128)(2,1)}, bf16[4,128,640]{2,1,0:T(8,128)(2,1)}, u32[]{:S(2)}, u32[]{:S(2)}) collective-permute-start(bf16[4,128,640]{2,1,0:T(8,128)(2,1)} %dynamic-slice_bitcast_fusion.6), channel_id=1, source_target_pairs={{0,16},{16,0},{1,17},{17,1},{2,18},{18,2},{3,19},{19,3},{4,20},{20... | collective-permute-start | bytes 1966088 | tf_op jit(solution)/shard_map/ppermute | solution.py:119
  279.0 221.6 %collective-permute-start.20 = (bf16[512,640]{1,0:T(8,128)(2,1)}, bf16[512,640]{1,0:T(8,128)(2,1)}, u32[]{:S(2)}, u32[]{:S(2)}) collective-permute-start(bf16[512,640]{1,0:T(8,128)(2,1)} %get-tuple-element.176), channel_id=1, source_target_pairs={{0,16},{16,0},{1,17},{17,1},{2,18},{18,2},{3,19},{19,3},{4,20},{20... | collective-permute-start | bytes 1966088 | tf_op jit(solution)/shard_map/ppermute | solution.py:119
  303.1 6.6 %collective-permute-start.28 = (bf16[4,96,1536]{2,1,0:T(8,128)(2,1)S(1)}, bf16[4,96,1536]{2,1,0:T(8,128)(2,1)S(1)}, u32[]{:S(2)}, u32[]{:S(2)}) collective-permute-start(bf16[4,96,1536]{2,1,0:T(8,128)(2,1)S(1)} %fusion.90), channel_id=1, source_target_pairs={{0,16},{16,0},{1,17},{17,1},{2,18},{18,2},{3,19},{19,3},{4,20},{20... | collective-permute-start | bytes 3538952 | tf_op jit(solution)/shard_map/ppermute | solution.py:119
  304.8 11.9 %collective-permute-start.31 = (bf16[2,128,640]{2,1,0:T(8,128)(2,1)S(1)}, bf16[2,128,640]{2,1,0:T(8,128)(2,1)S(1)}, u32[]{:S(2)}, u32[]{:S(2)}) collective-permute-start(bf16[2,128,640]{2,1,0:T(8,128)(2,1)S(1)} %pad_maximum_fusion.31), channel_id=1, source_target_pairs={{0,4},{4,0},{8,12},{12,8},{16,24},{20,28},{24,16},{28,20},{1,5},{5... | collective-permute-start | bytes 983048 | tf_op jit(solution)/shard_map/ppermute | solution.py:115
  309.3 10.7 %collective-permute-start.25 = (bf16[2,256,640]{2,1,0:T(8,128)(2,1)S(1)}, bf16[2,256,640]{2,1,0:T(8,128)(2,1)S(1)}, u32[]{:S(2)}, u32[]{:S(2)}) collective-permute-start(bf16[2,256,640]{2,1,0:T(8,128)(2,1)S(1)} %pad_maximum_fusion.19), channel_id=1, source_target_pairs={{0,4},{4,0},{8,12},{12,8},{16,24},{20,28},{24,16},{28,20},{1,5},{5... | collective-permute-start | bytes 1966088 | tf_op jit(solution)/shard_map/ppermute | solution.py:115
  311.1 15.1 %collective-permute-start.29 = (bf16[2,96,1536]{2,1,0:T(8,128)(2,1)S(1)}, bf16[2,96,1536]{2,1,0:T(8,128)(2,1)S(1)}, u32[]{:S(2)}, u32[]{:S(2)}) collective-permute-start(bf16[2,96,1536]{2,1,0:T(8,128)(2,1)S(1)} %pad_maximum_fusion.25), channel_id=1, source_target_pairs={{0,4},{4,0},{8,12},{12,8},{16,24},{20,28},{24,16},{28,20},{1,5},{5... | collective-permute-start | bytes 1769480 | tf_op jit(solution)/shard_map/ppermute | solution.py:115
  314.9 25.3 %collective-permute-start.23 = (bf16[2,80,4096]{2,1,0:T(8,128)(2,1)S(1)}, bf16[2,80,4096]{2,1,0:T(8,128)(2,1)S(1)}, u32[]{:S(2)}, u32[]{:S(2)}) collective-permute-start(bf16[2,80,4096]{2,1,0:T(8,128)(2,1)S(1)} %pad_maximum_fusion.16), channel_id=1, source_target_pairs={{0,4},{4,0},{8,12},{12,8},{16,24},{20,28},{24,16},{28,20},{1,5},{5... | collective-permute-start | bytes 3932168 | tf_op jit(solution)/shard_map/ppermute | solution.py:115
  365.1 80.2 %collective-permute-start.45 = (bf16[4,256,640]{2,1,0:T(8,128)(2,1)}, bf16[4,256,640]{2,1,0:T(8,128)(2,1)}, u32[]{:S(2)}, u32[]{:S(2)}) collective-permute-start(bf16[4,256,640]{2,1,0:T(8,128)(2,1)} %dynamic-slice_bitcast_fusion.2), channel_id=1, source_target_pairs={{0,16},{16,0},{1,17},{17,1},{2,18},{18,2},{3,19},{19,3},{4,20},{20... | collective-permute-start | bytes 3932168 | tf_op jit(solution)/shard_map/ppermute | solution.py:119
  366.9 85.0 %collective-permute-start.42 = (bf16[4,80,4096]{2,1,0:T(8,128)(2,1)}, bf16[4,80,4096]{2,1,0:T(8,128)(2,1)}, u32[]{:S(2)}, u32[]{:S(2)}) collective-permute-start(bf16[4,80,4096]{2,1,0:T(8,128)(2,1)} %dynamic-slice_bitcast_fusion), channel_id=1, source_target_pairs={{0,16},{16,0},{1,17},{17,1},{2,18},{18,2},{3,19},{19,3},{4,20},{20... | collective-permute-start | bytes 7864328 | tf_op jit(solution)/shard_map/ppermute | solution.py:119
  367.4 7.4 %collective-permute-start.27 = (bf16[256,640]{1,0:T(8,128)(2,1)}, bf16[256,640]{1,0:T(8,128)(2,1)}, u32[]{:S(2)}, u32[]{:S(2)}) collective-permute-start(bf16[256,640]{1,0:T(8,128)(2,1)} %get-tuple-element.65), channel_id=1, source_target_pairs={{0,8},{4,12},{8,0},{12,4},{16,20},{20,16},{24,28},{28,24},{1,9},{5... | collective-permute-start | bytes 983048 | tf_op jit(solution)/shard_map/ppermute | solution.py:115
  368.8 13.0 %collective-permute-start.26 = (bf16[80,4096]{1,0:T(8,128)(2,1)}, bf16[80,4096]{1,0:T(8,128)(2,1)}, u32[]{:S(2)}, u32[]{:S(2)}) collective-permute-start(bf16[80,4096]{1,0:T(8,128)(2,1)} %get-tuple-element.63), channel_id=1, source_target_pairs={{0,8},{4,12},{8,0},{12,4},{16,20},{20,16},{24,28},{28,24},{1,9},{5... | collective-permute-start | bytes 1966088 | tf_op jit(solution)/shard_map/ppermute | solution.py:115
  407.7 5.3 collective-permute-start.35
  410.1 7.0 %collective-permute-start.34 = (bf16[96,1536]{1,0:T(8,128)(2,1)}, bf16[96,1536]{1,0:T(8,128)(2,1)}, u32[]{:S(2)}, u32[]{:S(2)}) collective-permute-start(bf16[96,1536]{1,0:T(8,128)(2,1)} %get-tuple-element.68), channel_id=1, source_target_pairs={{0,8},{4,12},{8,0},{12,4},{16,20},{20,16},{24,28},{28,24},{1,9},{5... | collective-permute-start | bytes 884744 | tf_op jit(solution)/shard_map/ppermute | solution.py:115
  413.0 14.0 %collective-permute-start.32 = (bf16[512,512]{0,1:T(8,128)(2,1)}, bf16[512,512]{0,1:T(8,128)(2,1)}, u32[]{:S(2)}, u32[]{:S(2)}) collective-permute-start(bf16[512,512]{0,1:T(8,128)(2,1)} %pad_maximum_fusion.30), channel_id=1, source_target_pairs={{4,0},{8,4},{12,8},{5,1},{9,5},{13,9},{6,2},{10,6},{14,10},{7,3},{... | collective-permute-start | bytes 1572872 | tf_op jit(solution)/shard_map/ppermute | solution.py:20
  417.1 23.9 %collective-permute-start.39 = (bf16[4,128,640]{2,1,0:T(8,128)(2,1)}, bf16[4,128,640]{2,1,0:T(8,128)(2,1)}, u32[]{:S(2)}, u32[]{:S(2)}) collective-permute-start(bf16[4,128,640]{2,1,0:T(8,128)(2,1)} %dynamic-slice_bitcast_fusion.5), channel_id=1, source_target_pairs={{0,16},{16,0},{1,17},{17,1},{2,18},{18,2},{3,19},{19,3},{4,20},{20... | collective-permute-start | bytes 1966088 | tf_op jit(solution)/shard_map/ppermute | solution.py:119
  419.0 145.9 %all-reduce.17.cloned.1.call-start = ((), (), s32[]{:S(2)}) async-start(), calls=%async_computation | async-start | bytes 2883584 | tf_op jit(solution)/shard_map/psum | solution.py:538
  441.0 10.5 %collective-permute-start.36 = (bf16[4,96,1536]{2,1,0:T(8,128)(2,1)S(1)}, bf16[4,96,1536]{2,1,0:T(8,128)(2,1)S(1)}, u32[]{:S(2)}, u32[]{:S(2)}) collective-permute-start(bf16[4,96,1536]{2,1,0:T(8,128)(2,1)S(1)} %fusion.86), channel_id=1, source_target_pairs={{0,16},{16,0},{1,17},{17,1},{2,18},{18,2},{3,19},{19,3},{4,20},{20... | collective-permute-start | bytes 3538952 | tf_op jit(solution)/shard_map/ppermute | solution.py:119
  442.6 7.7 %collective-permute-start.40 = (bf16[2,128,640]{2,1,0:T(8,128)(2,1)S(1)}, bf16[2,128,640]{2,1,0:T(8,128)(2,1)S(1)}, u32[]{:S(2)}, u32[]{:S(2)}) collective-permute-start(bf16[2,128,640]{2,1,0:T(8,128)(2,1)S(1)} %pad_maximum_fusion.32), channel_id=1, source_target_pairs={{0,4},{4,0},{8,12},{12,8},{16,24},{20,28},{24,16},{28,20},{1,5},{5... | collective-permute-start | bytes 983048 | tf_op jit(solution)/shard_map/ppermute | solution.py:115
  447.2 12.4 %collective-permute-start.46 = (bf16[2,256,640]{2,1,0:T(8,128)(2,1)S(1)}, bf16[2,256,640]{2,1,0:T(8,128)(2,1)S(1)}, u32[]{:S(2)}, u32[]{:S(2)}) collective-permute-start(bf16[2,256,640]{2,1,0:T(8,128)(2,1)S(1)} %pad_maximum_fusion.20), channel_id=1, source_target_pairs={{0,4},{4,0},{8,12},{12,8},{16,24},{20,28},{24,16},{28,20},{1,5},{5... | collective-permute-start | bytes 1966088 | tf_op jit(solution)/shard_map/ppermute | solution.py:115
  450.4 7.2 %collective-permute-start.41 = (bf16[128,640]{1,0:T(8,128)(2,1)S(1)}, bf16[128,640]{1,0:T(8,128)(2,1)S(1)}, u32[]{:S(2)}, u32[]{:S(2)}) collective-permute-start(bf16[128,640]{1,0:T(8,128)(2,1)S(1)} %fusion.191), channel_id=1, source_target_pairs={{0,8},{4,12},{8,0},{12,4},{16,20},{20,16},{24,28},{28,24},{1,9},{5... | collective-permute-start | bytes 491528 | tf_op jit(solution)/shard_map/ppermute | solution.py:115
  454.9 29.3 %collective-permute-start.43 = (bf16[2,80,4096]{2,1,0:T(8,128)(2,1)S(1)}, bf16[2,80,4096]{2,1,0:T(8,128)(2,1)S(1)}, u32[]{:S(2)}, u32[]{:S(2)}) collective-permute-start(bf16[2,80,4096]{2,1,0:T(8,128)(2,1)S(1)} %pad_maximum_fusion.17), channel_id=1, source_target_pairs={{0,4},{4,0},{8,12},{12,8},{16,24},{20,28},{24,16},{28,20},{1,5},{5... | collective-permute-start | bytes 3932168 | tf_op jit(solution)/shard_map/ppermute | solution.py:115
  456.1 27.3 %collective-permute-start.37 = (bf16[2,96,1536]{2,1,0:T(8,128)(2,1)S(1)}, bf16[2,96,1536]{2,1,0:T(8,128)(2,1)S(1)}, u32[]{:S(2)}, u32[]{:S(2)}) collective-permute-start(bf16[2,96,1536]{2,1,0:T(8,128)(2,1)S(1)} %pad_maximum_fusion.26), channel_id=1, source_target_pairs={{0,4},{4,0},{8,12},{12,8},{16,24},{20,28},{24,16},{28,20},{1,5},{5... | collective-permute-start | bytes 1769480 | tf_op jit(solution)/shard_map/ppermute | solution.py:115
  459.8 26.5 %collective-permute-start.47 = (bf16[256,640]{1,0:T(8,128)(2,1)S(1)}, bf16[256,640]{1,0:T(8,128)(2,1)S(1)}, u32[]{:S(2)}, u32[]{:S(2)}) collective-permute-start(bf16[256,640]{1,0:T(8,128)(2,1)S(1)} %fusion.148), channel_id=1, source_target_pairs={{0,8},{4,12},{8,0},{12,4},{16,20},{20,16},{24,28},{28,24},{1,9},{5... | collective-permute-start | bytes 983048 | tf_op jit(solution)/shard_map/ppermute | solution.py:115
  483.7 6.8 %collective-permute-start.38 = (bf16[96,1536]{1,0:T(8,128)(2,1)S(1)}, bf16[96,1536]{1,0:T(8,128)(2,1)S(1)}, u32[]{:S(2)}, u32[]{:S(2)}) collective-permute-start(bf16[96,1536]{1,0:T(8,128)(2,1)S(1)} %fusion.156), channel_id=1, source_target_pairs={{0,8},{4,12},{8,0},{12,4},{16,20},{20,16},{24,28},{28,24},{1,9},{5... | collective-permute-start | bytes 884744 | tf_op jit(solution)/shard_map/ppermute | solution.py:115
  484.6 12.9 %collective-permute-start.44 = (bf16[80,4096]{1,0:T(8,128)(2,1)S(1)}, bf16[80,4096]{1,0:T(8,128)(2,1)S(1)}, u32[]{:S(2)}, u32[]{:S(2)}) collective-permute-start(bf16[80,4096]{1,0:T(8,128)(2,1)S(1)} %fusion.98), channel_id=1, source_target_pairs={{0,8},{4,12},{8,0},{12,4},{16,20},{20,16},{24,28},{28,24},{1,9},{5... | collective-permute-start | bytes 1966088 | tf_op jit(solution)/shard_map/ppermute | solution.py:115
  500.5 2.6 collective-permute-start.33
  503.4 61.6 %copy-start.90 = (bf16[256,640]{1,0:T(8,128)(2,1)S(1)}, bf16[256,640]{1,0:T(8,128)(2,1)}, u32[]{:S(2)}) copy-start(bf16[256,640]{1,0:T(8,128)(2,1)} %get-tuple-element.80) | copy-start | bytes 983044
  503.4 61.7 %copy-start.75 = (bf16[80,4096]{1,0:T(8,128)(2,1)S(1)}, bf16[80,4096]{1,0:T(8,128)(2,1)}, u32[]{:S(2)}) copy-start(bf16[80,4096]{1,0:T(8,128)(2,1)} %get-tuple-element.78) | copy-start | bytes 1966084
  505.0 61.8 %copy-start.113 = (bf16[128,640]{1,0:T(8,128)(2,1)S(1)}, bf16[128,640]{1,0:T(8,128)(2,1)}, u32[]{:S(2)}) copy-start(bf16[128,640]{1,0:T(8,128)(2,1)} %get-tuple-element.76) | copy-start | bytes 491524
  505.0 62.5 %copy-start.127 = (bf16[96,1536]{1,0:T(8,128)(2,1)S(1)}, bf16[96,1536]{1,0:T(8,128)(2,1)}, u32[]{:S(2)}) copy-start(bf16[96,1536]{1,0:T(8,128)(2,1)} %get-tuple-element.74) | copy-start | bytes 884740
  565.0 8.8 %collective-permute-start.51 = (bf16[256,640]{1,0:T(8,128)(2,1)S(1)}, bf16[256,640]{1,0:T(8,128)(2,1)}, u32[]{:S(2)}, u32[]{:S(2)}) collective-permute-start(bf16[256,640]{1,0:T(8,128)(2,1)S(1)} %broadcast_select_fusion.5), channel_id=1, source_target_pairs={{0,16},{16,0},{1,17},{17,1},{2,18},{18,2},{3,19},{19,3},{4,20},{20... | collective-permute-start | bytes 983048 | tf_op jit(solution)/shard_map/ppermute | solution.py:119
  565.2 10.8 %collective-permute-start.50 = (bf16[80,4096]{1,0:T(8,128)(2,1)S(1)}, bf16[80,4096]{1,0:T(8,128)(2,1)S(1)}, u32[]{:S(2)}, u32[]{:S(2)}) collective-permute-start(bf16[80,4096]{1,0:T(8,128)(2,1)S(1)} %broadcast_select_fusion), channel_id=1, source_target_pairs={{0,16},{16,0},{1,17},{17,1},{2,18},{18,2},{3,19},{19,3},{4,20},{20... | collective-permute-start | bytes 1966088 | tf_op jit(solution)/shard_map/ppermute | solution.py:119
  567.5 2.6 collective-permute-start.49
  568.3 3.7 collective-permute-start.48
  (202 other events, 1067.6 us)
Sparse Core Ops, SparseCore 0:
  419.2 68.3 all-reduce.18
  498.6 66.2 all-reduce.16
